TPU v7x, 256 devices: a whole 4x4x8 slice. The times are simulated.
256 devices in a mesh: tbl: 64 (over z, y, core), tm: 4 (over x).
Axes of the slice: x: 4, y: 4, z: 8, core: 2. Of those that a mesh axis runs over, the one named last changes fastest.
Arguments:
- table: bfloat16 [2097152, 128], P('tbl'), may hold values from -64 to 64
- fetch_rows: int32 [64, 4, 64, 512], P('tbl', 'tm'), may hold values from 0 to 32767
- tile_counts: int32 [64, 4, 64], P('tbl', 'tm'), may hold values from 1 to 4, as said below
- hist_source: int32 [64, 4, 2, 8192], P('tbl', 'tm'), may hold values from 0 to 32767, as said below
- cand_source: int32 [64, 4, 512], P('tbl', 'tm'), may hold values from 0 to 32767, as said below
- lengths: int32 [64, 2], P('tbl'), may hold values from 1 to 32768
- w_query: bfloat16 [128, 128], replicated, may hold values from -0.5 to 0.5
- w_key: bfloat16 [128, 128], replicated, may hold values from -0.5 to 0.5
- w_value: bfloat16 [128, 128], replicated, may hold values from -0.5 to 0.5
- w_out: bfloat16 [128, 128], replicated, may hold values from -0.5 to 0.5
Outputs:
- interest: bfloat16 [131072, 128], P(('tbl', 'tm'))
Inputs may be any that keep to these rules, and one draw needn't show every extreme that they name: `tile_counts`: in every draw some owner is asked for 4 tiles by every device, and on every device at least one owner has 4 live tiles. `hist_source`: every entry names a slot in a tile that tile_counts counts live for that device and owner. On every device all 512 slots of some owner are named. `cand_source`: every entry names a slot in a tile that tile_counts counts live for that device and owner.
All inputs are finite; a program needn't handle non-finite values.
Results may differ from a plain program's by a relative error of at most 0.0059.
The roundings to bfloat16 on the way count: a program that leaves them out, or rounds other values in their place, can miss the bound.
Values may be sent and summed in bfloat16 or wider, within the bound.
A program may use at most 128 MiB of HBM per device.

v0:
```python
import math

import jax
import jax.numpy as jnp
from jax import lax
from jax.sharding import PartitionSpec as P

HEADS = 4
TILE = 128


NEG_FILL = -1e30


def joined(array, axis, combine):
    everything = jax.tree.map(lambda part: lax.all_gather(part, axis), array)
    leading = jax.tree.map(lambda part: part[0], everything)

    def hop(k, so_far):
        return combine(so_far, jax.tree.map(lambda part: part[k], everything))

    return lax.fori_loop(1, lax.axis_size(axis), hop, leading)


def fold_partials(former, latter):
    joined_peak = jnp.maximum(former[0], latter[0])
    former_w = jnp.exp(former[0] - joined_peak)
    latter_w = jnp.exp(latter[0] - joined_peak)
    row_count = former[2].shape[0]
    head_count = former[0].shape[1]
    former_acc = former[2].reshape(row_count, head_count, -1) * former_w[:, :, None]
    latter_acc = latter[2].reshape(row_count, head_count, -1) * latter_w[:, :, None]
    joined_acc = (former_acc + latter_acc).reshape(row_count, -1)
    return (joined_peak, former[1] * former_w + latter[1] * latter_w, joined_acc)


def shards(
    table,
    fetch_rows,
    tile_counts,
    hist_source,
    cand_source,
    lengths,
    w_query,
    w_key,
    w_value,
    w_out,
):
    owner_count = fetch_rows.shape[2]
    capacity = fetch_rows.shape[3]
    embed_width = table.shape[1]
    head_count = HEADS
    head_dim = embed_width // head_count
    tile_ids = fetch_rows[0, 0].reshape(owner_count, capacity // TILE, TILE)
    looked = jnp.take(
        table, lax.all_to_all(tile_ids, "tbl", split_axis=0, concat_axis=0, tiled=True), axis=0
    )
    fetched = lax.all_to_all(looked, "tbl", split_axis=0, concat_axis=0, tiled=True)
    tile_index = jnp.arange(capacity // TILE, dtype=jnp.int32)
    counted = tile_index[None, :] < tile_counts[0, 0][:, None]
    fetched = jnp.where(counted[:, :, None, None], fetched, jnp.zeros((), fetched.dtype))
    flat_rows = fetched.reshape(owner_count * capacity, embed_width)
    history = jnp.take(flat_rows, hist_source[0, 0].reshape(-1), axis=0)
    own_cands = jnp.take(flat_rows, cand_source[0, 0], axis=0)
    cand_dev = own_cands.shape[0]
    both_weights = jnp.concatenate((w_key, w_value), axis=1)
    projected = jnp.dot(history, both_weights, preferred_element_type=jnp.float32).astype(
        jnp.bfloat16
    )
    requests = lengths.shape[1]
    slice_len = hist_source.shape[3]
    keys_all = projected[:, :embed_width].reshape(requests, slice_len, head_count, head_dim)
    values_all = projected[:, embed_width:].reshape(requests, slice_len, head_count, head_dim)
    group_cands = lax.all_gather(own_cands, "tm", axis=0, tiled=True)
    queries = jnp.dot(group_cands, w_query, preferred_element_type=jnp.float32).astype(jnp.bfloat16)
    cands_per = queries.shape[0] // requests
    block_rows = min(128, cands_per)
    block_count = cands_per // block_rows
    queries = queries.reshape(requests, block_count, block_rows, head_count, head_dim)
    slice_pos = lax.axis_index("tm")
    live_all = lengths[0] - slice_pos * slice_len
    score_scale = 1.0 / math.sqrt(head_dim)

    def attend(operands):
        query_blocks, keys_one, values_one, live_len = operands
        visible = jnp.arange(keys_one.shape[0], dtype=jnp.int32) < live_len

        def one_block(query_one):
            scores = (
                jnp.einsum("chd,phd->hcp", query_one, keys_one, preferred_element_type=jnp.float32)
                * score_scale
            )
            masked = jnp.where(visible, scores, NEG_FILL)
            peak_score = jnp.max(masked, axis=2)
            weights = jnp.where(visible, jnp.exp(masked - peak_score[:, :, None]), 0.0).astype(
                jnp.bfloat16
            )
            weight_sum = jnp.sum(weights, axis=2, dtype=jnp.float32)
            summed = jnp.einsum(
                "hcp,phd->chd", weights, values_one, preferred_element_type=jnp.float32
            )
            return (peak_score.T, weight_sum.T, summed.reshape(summed.shape[0], embed_width))

        peaks, sums, numers = lax.map(one_block, query_blocks)
        return (
            peaks.reshape(cands_per, head_count),
            sums.reshape(cands_per, head_count),
            numers.reshape(cands_per, embed_width),
        )

    def one_request(operands):
        return attend(operands)

    peak_all, totals, numerators = lax.map(one_request, (queries, keys_all, values_all, live_all))
    row_count = requests * cands_per
    peak_all = peak_all.reshape(row_count, head_count)
    totals = totals.reshape(row_count, head_count)
    numerators = numerators.reshape(row_count, embed_width)
    merged = joined((peak_all, totals, numerators), "tm", fold_partials)
    own_start = slice_pos * cand_dev
    own_total = lax.dynamic_slice_in_dim(merged[1], own_start, cand_dev, 0)
    own_sum = lax.dynamic_slice_in_dim(merged[2], own_start, cand_dev, 0)
    attended = (
        (own_sum.reshape(cand_dev, head_count, head_dim) / own_total[:, :, None])
        .reshape(cand_dev, embed_width)
        .astype(jnp.bfloat16)
    )
    return jnp.dot(attended, w_out, preferred_element_type=jnp.float32).astype(jnp.bfloat16)


def solution(mesh):
    return jax.shard_map(
        shards,
        mesh=mesh,
        in_specs=(
            P("tbl", None),
            P("tbl", "tm", None, None),
            P("tbl", "tm", None),
            P("tbl", "tm", None, None),
            P("tbl", "tm", None),
            P("tbl", None),
            P(),
            P(),
            P(),
            P(),
        ),
        out_specs=P(("tbl", "tm"), None),
        check_vma=False,
    )
```

profile of v0, /device:TPU:32, one launch (start us, length us, event | category | flops | bytes accessed | tf_op | source)
XLA Modules:
  0.0 878.3 jit_solution(4219067045874318925)
XLA Ops:
  7.5 21.7 %all_to_all.10 = s32[64,4,128]{2,1,0:T(4,128)S(1)} all-to-all(s32[64,4,128]{2,1,0:T(4,128)S(1)} %reshape_squeeze.8), channel_id=1, replica_groups=mesh['tbl'=64,'tm'=4] {'tbl'}, dimensions={0} | all-to-all | bytes 262144 | tf_op jit(solution)/shard_map/all_to_all | solution.py:56
  29.3 114.7 %gather_fusion = bf16[32768,128]{1,0:T(8,128)(2,1)} fusion(bf16[32768,128]{1,0:T(8,128)(2,1)} %param.16, s32[32768]{0:T(1024)S(1)} %broadcast_clamp_fusion), kind=kCustom, calls=%fused_computation | custom fusion | bytes 16908288 | tf_op jit(solution)/shard_map/jit(_take)/gather | solution.py:55
  158.8 185.9 %all-to-all-done.1 = bf16[64,4,128,128]{3,2,1,0:T(8,128)(2,1)} async-done(((bf16[64,4,128,128]{3,2,1,0:T(8,128)(2,1)}), bf16[64,4,128,128]{3,2,1,0:T(8,128)(2,1)}, u32[]{:S(2)}, u32[]{:S(2)}) %all-to-all-start.1) | async-done | bytes 8388640 | tf_op jit(solution)/shard_map/all_to_all | solution.py:58
  357.7 13.3 %all_gather.12 = bf16[2048,128]{1,0:T(8,128)(2,1)S(1)} all-gather(bf16[512,128]{1,0:T(8,128)(2,1)S(1)} %broadcast_select_fusion.2), channel_id=1, replica_groups=mesh['tbl'=64,'tm'=4] {'tm'}, dimensions={0}, use_global_device_ids=true | all-gather | bytes 655360 | tf_op jit(solution)/shard_map/all_gather | solution.py:74
  372.4 59.8 %gather_fusion.2 = bf16[16384,128]{1,0:T(8,128)(2,1)} fusion(bf16[32768,128]{1,0:T(8,128)(2,1)} %bitcast.130, s32[16384]{0:T(1024)S(1)} %broadcast_clamp_fusion.1), kind=kCustom, calls=%fused_computation.2 | custom fusion | bytes 8454144 | tf_op jit(solution)/shard_map/jit(_take)/gather | solution.py:63
  487.7 325.0 %while.49 = (s32[]{:T(128)}, f32[2,1024,4]{1,2,0:T(4,128)S(1)}, f32[2,1024,4]{1,2,0:T(4,128)S(1)}, f32[2,1024,128]{2,1,0:T(8,128)}, bf16[2,8,128,4,32]{2,1,0,4,3...) while((s32[]{:T(128)}, f32[2,1024,4]{1,2,0:T(4,128)S(1)}, ...), condition=%wide.region_5.6_spmd, body=%wide.region_0.5_spmd.sunk | while | flops 599792640 | bytes 132596080 | solution.py:114
  493.4 156.0 %while.51 = (s32[]{:T(128)}, f32[8,128,4]{1,2,0:T(4,128)S(1)}, f32[8,128,4]{1,2,0:T(4,128)S(1)}, f32[8,128,128]{2,1,0:T(8,128)S(1)}, bf16[8,128,4,32]{1,3,2,0:T(...) while((s32[]{:T(128)}, f32[8,128,4]{1,2,0:T(4,128)S(1)}, ...), condition=%wide.region_4.4_spmd.clone, body=%wide.region_1.3_spmd.clone.sunk | while | flops 599792640 | bytes 122044560 | solution.py:104
  522.0 10.2 %fusion.39 = f32[4,128,32]{1,2,0:T(8,128)S(1)} fusion(bf16[8192,4,32]{0,2,1:T(8,128)(2,1)} %get-tuple-element.591, f32[4,128,8192]{2,1,0:T(8,128)} %copy-done.2, f32[4,128]{1,0:T(4,128)S(1)} %get-tuple-element.563, pred[8192]{0:T(1024)(128)(4,1)S(1)} %iota_compare_fusion.3), kind=kOutput, calls=%fused_computation.26.clone.1 | convolution fusion | flops 289406976 | bytes 18950144 | tf_op jit(solution)/shard_map/while/body/eval_jaxpr/while/body/eval_jaxpr/hcp,phd->chd/dot_general | solution.py:99
  541.5 10.2 %fusion.39 = f32[4,128,32]{1,2,0:T(8,128)S(1)} fusion(bf16[8192,4,32]{0,2,1:T(8,128)(2,1)} %get-tuple-element.591, f32[4,128,8192]{2,1,0:T(8,128)} %copy-done.2, f32[4,128]{1,0:T(4,128)S(1)} %get-tuple-element.563, pred[8192]{0:T(1024)(128)(4,1)S(1)} %iota_compare_fusion.3), kind=kOutput, calls=%fused_computation.26.clone.1 | convolution fusion | flops 289406976 | bytes 18950144 | tf_op jit(solution)/shard_map/while/body/eval_jaxpr/while/body/eval_jaxpr/hcp,phd->chd/dot_general | solution.py:99
  561.0 10.2 %fusion.39 = f32[4,128,32]{1,2,0:T(8,128)S(1)} fusion(bf16[8192,4,32]{0,2,1:T(8,128)(2,1)} %get-tuple-element.591, f32[4,128,8192]{2,1,0:T(8,128)} %copy-done.2, f32[4,128]{1,0:T(4,128)S(1)} %get-tuple-element.563, pred[8192]{0:T(1024)(128)(4,1)S(1)} %iota_compare_fusion.3), kind=kOutput, calls=%fused_computation.26.clone.1 | convolution fusion | flops 289406976 | bytes 18950144 | tf_op jit(solution)/shard_map/while/body/eval_jaxpr/while/body/eval_jaxpr/hcp,phd->chd/dot_general | solution.py:99
  580.5 10.2 %fusion.39 = f32[4,128,32]{1,2,0:T(8,128)S(1)} fusion(bf16[8192,4,32]{0,2,1:T(8,128)(2,1)} %get-tuple-element.591, f32[4,128,8192]{2,1,0:T(8,128)} %copy-done.2, f32[4,128]{1,0:T(4,128)S(1)} %get-tuple-element.563, pred[8192]{0:T(1024)(128)(4,1)S(1)} %iota_compare_fusion.3), kind=kOutput, calls=%fused_computation.26.clone.1 | convolution fusion | flops 289406976 | bytes 18950144 | tf_op jit(solution)/shard_map/while/body/eval_jaxpr/while/body/eval_jaxpr/hcp,phd->chd/dot_general | solution.py:99
  600.0 10.2 %fusion.39 = f32[4,128,32]{1,2,0:T(8,128)S(1)} fusion(bf16[8192,4,32]{0,2,1:T(8,128)(2,1)} %get-tuple-element.591, f32[4,128,8192]{2,1,0:T(8,128)} %copy-done.2, f32[4,128]{1,0:T(4,128)S(1)} %get-tuple-element.563, pred[8192]{0:T(1024)(128)(4,1)S(1)} %iota_compare_fusion.3), kind=kOutput, calls=%fused_computation.26.clone.1 | convolution fusion | flops 289406976 | bytes 18950144 | tf_op jit(solution)/shard_map/while/body/eval_jaxpr/while/body/eval_jaxpr/hcp,phd->chd/dot_general | solution.py:99
  619.5 10.2 %fusion.39 = f32[4,128,32]{1,2,0:T(8,128)S(1)} fusion(bf16[8192,4,32]{0,2,1:T(8,128)(2,1)} %get-tuple-element.591, f32[4,128,8192]{2,1,0:T(8,128)} %copy-done.2, f32[4,128]{1,0:T(4,128)S(1)} %get-tuple-element.563, pred[8192]{0:T(1024)(128)(4,1)S(1)} %iota_compare_fusion.3), kind=kOutput, calls=%fused_computation.26.clone.1 | convolution fusion | flops 289406976 | bytes 18950144 | tf_op jit(solution)/shard_map/while/body/eval_jaxpr/while/body/eval_jaxpr/hcp,phd->chd/dot_general | solution.py:99
  639.0 10.2 %fusion.39 = f32[4,128,32]{1,2,0:T(8,128)S(1)} fusion(bf16[8192,4,32]{0,2,1:T(8,128)(2,1)} %get-tuple-element.591, f32[4,128,8192]{2,1,0:T(8,128)} %copy-done.2, f32[4,128]{1,0:T(4,128)S(1)} %get-tuple-element.563, pred[8192]{0:T(1024)(128)(4,1)S(1)} %iota_compare_fusion.3), kind=kOutput, calls=%fused_computation.26.clone.1 | convolution fusion | flops 289406976 | bytes 18950144 | tf_op jit(solution)/shard_map/while/body/eval_jaxpr/while/body/eval_jaxpr/hcp,phd->chd/dot_general | solution.py:99
  655.8 156.0 %while.51 = (s32[]{:T(128)}, f32[8,128,4]{1,2,0:T(4,128)S(1)}, f32[8,128,4]{1,2,0:T(4,128)S(1)}, f32[8,128,128]{2,1,0:T(8,128)S(1)}, bf16[8,128,4,32]{1,3,2,0:T(...) while((s32[]{:T(128)}, f32[8,128,4]{1,2,0:T(4,128)S(1)}, ...), condition=%wide.region_4.4_spmd.clone, body=%wide.region_1.3_spmd.clone.sunk | while | flops 599792640 | bytes 122044560 | solution.py:104
  704.0 10.2 %fusion.39 = f32[4,128,32]{1,2,0:T(8,128)S(1)} fusion(bf16[8192,4,32]{0,2,1:T(8,128)(2,1)} %get-tuple-element.591, f32[4,128,8192]{2,1,0:T(8,128)} %copy-done.2, f32[4,128]{1,0:T(4,128)S(1)} %get-tuple-element.563, pred[8192]{0:T(1024)(128)(4,1)S(1)} %iota_compare_fusion.3), kind=kOutput, calls=%fused_computation.26.clone.1 | convolution fusion | flops 289406976 | bytes 18950144 | tf_op jit(solution)/shard_map/while/body/eval_jaxpr/while/body/eval_jaxpr/hcp,phd->chd/dot_general | solution.py:99
  723.5 10.2 %fusion.39 = f32[4,128,32]{1,2,0:T(8,128)S(1)} fusion(bf16[8192,4,32]{0,2,1:T(8,128)(2,1)} %get-tuple-element.591, f32[4,128,8192]{2,1,0:T(8,128)} %copy-done.2, f32[4,128]{1,0:T(4,128)S(1)} %get-tuple-element.563, pred[8192]{0:T(1024)(128)(4,1)S(1)} %iota_compare_fusion.3), kind=kOutput, calls=%fused_computation.26.clone.1 | convolution fusion | flops 289406976 | bytes 18950144 | tf_op jit(solution)/shard_map/while/body/eval_jaxpr/while/body/eval_jaxpr/hcp,phd->chd/dot_general | solution.py:99
  743.0 10.2 %fusion.39 = f32[4,128,32]{1,2,0:T(8,128)S(1)} fusion(bf16[8192,4,32]{0,2,1:T(8,128)(2,1)} %get-tuple-element.591, f32[4,128,8192]{2,1,0:T(8,128)} %copy-done.2, f32[4,128]{1,0:T(4,128)S(1)} %get-tuple-element.563, pred[8192]{0:T(1024)(128)(4,1)S(1)} %iota_compare_fusion.3), kind=kOutput, calls=%fused_computation.26.clone.1 | convolution fusion | flops 289406976 | bytes 18950144 | tf_op jit(solution)/shard_map/while/body/eval_jaxpr/while/body/eval_jaxpr/hcp,phd->chd/dot_general | solution.py:99
  762.5 10.2 %fusion.39 = f32[4,128,32]{1,2,0:T(8,128)S(1)} fusion(bf16[8192,4,32]{0,2,1:T(8,128)(2,1)} %get-tuple-element.591, f32[4,128,8192]{2,1,0:T(8,128)} %copy-done.2, f32[4,128]{1,0:T(4,128)S(1)} %get-tuple-element.563, pred[8192]{0:T(1024)(128)(4,1)S(1)} %iota_compare_fusion.3), kind=kOutput, calls=%fused_computation.26.clone.1 | convolution fusion | flops 289406976 | bytes 18950144 | tf_op jit(solution)/shard_map/while/body/eval_jaxpr/while/body/eval_jaxpr/hcp,phd->chd/dot_general | solution.py:99
  782.0 10.2 %fusion.39 = f32[4,128,32]{1,2,0:T(8,128)S(1)} fusion(bf16[8192,4,32]{0,2,1:T(8,128)(2,1)} %get-tuple-element.591, f32[4,128,8192]{2,1,0:T(8,128)} %copy-done.2, f32[4,128]{1,0:T(4,128)S(1)} %get-tuple-element.563, pred[8192]{0:T(1024)(128)(4,1)S(1)} %iota_compare_fusion.3), kind=kOutput, calls=%fused_computation.26.clone.1 | convolution fusion | flops 289406976 | bytes 18950144 | tf_op jit(solution)/shard_map/while/body/eval_jaxpr/while/body/eval_jaxpr/hcp,phd->chd/dot_general | solution.py:99
  801.5 10.2 %fusion.39 = f32[4,128,32]{1,2,0:T(8,128)S(1)} fusion(bf16[8192,4,32]{0,2,1:T(8,128)(2,1)} %get-tuple-element.591, f32[4,128,8192]{2,1,0:T(8,128)} %copy-done.2, f32[4,128]{1,0:T(4,128)S(1)} %get-tuple-element.563, pred[8192]{0:T(1024)(128)(4,1)S(1)} %iota_compare_fusion.3), kind=kOutput, calls=%fused_computation.26.clone.1 | convolution fusion | flops 289406976 | bytes 18950144 | tf_op jit(solution)/shard_map/while/body/eval_jaxpr/while/body/eval_jaxpr/hcp,phd->chd/dot_general | solution.py:99
  812.7 12.1 %all_gather.13 = f32[4,2048,4]{1,2,0:T(4,128)S(1)} all-gather(f32[1,2048,4]{1,2,0:T(4,128)S(1)} %bitcast.142), channel_id=1, replica_groups=mesh['tbl'=64,'tm'=4] {'tm'}, dimensions={0}, use_global_device_ids=true | all-gather | bytes 163840 | tf_op jit(solution)/shard_map/all_gather | solution.py:16
  824.8 12.4 %all_gather.14 = f32[4,2048,4]{1,2,0:T(4,128)S(1)} all-gather(f32[1,2048,4]{1,2,0:T(4,128)S(1)} %bitcast.143), channel_id=1, replica_groups=mesh['tbl'=64,'tm'=4] {'tm'}, dimensions={0}, use_global_device_ids=true | all-gather | bytes 163840 | tf_op jit(solution)/shard_map/all_gather | solution.py:16
  837.3 24.3 %all-gather.2.cloned.1.call-done = f32[4,2048,128]{2,1,0:T(8,128)} async-done(((f32[1,2048,128]{2,1,0:T(8,128)}), f32[4,2048,128]{2,1,0:T(8,128)}) %all-gather.2.cloned.1.call-update) | async-done | bytes 4194320 | tf_op jit(solution)/shard_map/all_gather | solution.py:16
  (222 shorter events, 293.5 us)
Async XLA Ops:
  6.5 364.5 %copy-start = (bf16[128,128]{1,0:T(8,128)(2,1)S(1)}, bf16[128,128]{1,0:T(8,128)(2,1)}, u32[]{:S(2)}) copy-start(bf16[128,128]{1,0:T(8,128)(2,1)} %param.22) | copy-start | bytes 98308
  151.7 6.8 copy-start.3
  151.7 6.9 copy-start.6
  151.7 6.9 copy-start.8
  151.7 6.9 copy-start.7
  151.7 193.0 %all-to-all-start.1 = ((bf16[64,4,128,128]{3,2,1,0:T(8,128)(2,1)}), bf16[64,4,128,128]{3,2,1,0:T(8,128)(2,1)}, u32[]{:S(2)}, u32[]{:S(2)}) async-start(bf16[64,4,128,128]{3,2,1,0:T(8,128)(2,1)} %broadcast_select_fusion), calls=%async_computation.1 | async-start | bytes 16777216 | tf_op jit(solution)/shard_map/all_to_all | solution.py:58
  158.4 703.2 %all-gather.2.cloned.1.call-start = ((), (), s32[]{:S(2)}) async-start(), calls=%async_computation.2 | async-start | bytes 5242880 | tf_op jit(solution)/shard_map/all_gather | solution.py:16
  372.4 59.8 %copy-start.4 = (bf16[128,128]{1,0:T(8,128)(2,1)S(1)}, bf16[128,128]{1,0:T(8,128)(2,1)}, u32[]{:S(2)}) copy-start(bf16[128,128]{1,0:T(8,128)(2,1)} %param.24) | copy-start | bytes 98308
  372.4 59.8 %copy-start.5 = (bf16[128,128]{1,0:T(8,128)(2,1)S(1)}, bf16[128,128]{1,0:T(8,128)(2,1)}, u32[]{:S(2)}) copy-start(bf16[128,128]{1,0:T(8,128)(2,1)} %param.23) | copy-start | bytes 98308
  496.8 5.8 copy-start.2
  516.3 5.8 copy-start.2
  535.8 5.8 copy-start.2
  555.3 5.8 copy-start.2
  574.8 5.8 copy-start.2
  594.3 5.8 copy-start.2
  613.8 5.8 copy-start.2
  633.3 5.8 copy-start.2
  659.2 5.8 copy-start.2
  678.7 5.8 copy-start.2
  698.2 5.8 copy-start.2
  717.7 5.8 copy-start.2
  737.2 5.8 copy-start.2
  756.7 5.8 copy-start.2
  776.2 5.8 copy-start.2
  (2 other events, 7.4 us)
Sparse Core Ops, SparseCore 0:
  812.8 48.6 all-gather.1
where the time goes:
time: 881 us; the launch traced here: 878 us
  local copies, waits for them, and re-layouts  258 us (29%)
  matrix products  219 us (25%)
  waiting for transfers between devices  210 us (24%)
  other arithmetic  110 us (12%)
  blocking collectives  59.6 us (7%)
  between operations  13.7 us (2%)
    all_to_all x1, waiting for transfers between devices, shards(): lax.all_to_all(looked, 'tbl', split_axis=0, concat_axis=0, tiled=True)  186 us
    dot_general x16, matrix products, one_block(): jnp.einsum('hcp,phd->chd', weights, values_one, preferred_element_type=jn...  163 us
    gather x1, local copies, waits for them, and re-layouts, shards(): jnp.take(table, lax.all_to_all(tile_ids, 'tbl', split_axis=0, concat_axis...  115 us
    reduce_sum x16, other arithmetic, one_block(): weight_sum = jnp.sum(weights, axis=2, dtype=jnp.float32)  83.2 us
    gather x1, local copies, waits for them, and re-layouts, shards(): history = jnp.take(flat_rows, hist_source[0, 0].reshape(-1), axis=0)  59.8 us
    dot_general x16, matrix products, one_block(): jnp.einsum('chd,phd->hcp', query_one, keys_one, preferred_element_type=jn...  44.2 us
    all_gather x2, blocking collectives, joined(): everything = jax.tree.map(lambda part: lax.all_gather(part, axis), array)  24.5 us
    all_gather x1, waiting for transfers between devices, joined(): everything = jax.tree.map(lambda part: lax.all_gather(part, axis), array)  24.3 us
  transfers between devices with their start and end apart: 2, of which 2 were waited for; matrix products, arithmetic and copies ran while one was open for 0% of the time, Pallas kernels for 0%

commit v1 on v0

v1 whole, which is shorter than its diff:
```python
import functools
import math

import jax
import jax.numpy as jnp
from jax import lax
from jax.experimental import pallas as pl
from jax.experimental.pallas import tpu as pltpu
from jax.sharding import PartitionSpec as P

HEADS = 4
TILE = 128
HEAD_ROWS = 48
PART_ROWS = 40
ROW_STEP = 2048
SUB = 256
GATHER_STEP = 256
VMEM_LIMIT = 58 << 20
NEG_FILL = -1e30

VMEM = pl.BlockSpec(memory_space=pltpu.VMEM)
SMEM = pl.BlockSpec(memory_space=pltpu.SMEM)


def owner_gather_kernel(chunk, asked, table, out, wide, rows_wide):
    devices, capacity = out.shape[0], asked.shape[0] // out.shape[0]
    step = 1024

    def widen(i, carry):
        rows = pl.ds(pl.multiple_of(i * step, step), step)
        wide[rows, :] = table[rows, :].astype(jnp.float32)
        return carry

    lax.fori_loop(0, table.shape[0] // step, widen, 0)

    def one_device(d, carry):
        base = d * capacity + chunk * TILE
        for j in range(TILE):
            rows_wide[j : j + 1, :] = wide[pl.ds(asked[base + j], 1), :]
        out[d] = rows_wide[...].astype(out.dtype)
        return carry

    lax.fori_loop(0, devices, one_device, 0)


def owner_gather(chunk, asked, table, devices):
    return pl.pallas_call(
        functools.partial(owner_gather_kernel, chunk),
        out_shape=jax.ShapeDtypeStruct((devices, TILE, table.shape[1]), table.dtype),
        in_specs=[SMEM, VMEM],
        out_specs=VMEM,
        scratch_shapes=[
            pltpu.VMEM(table.shape, jnp.float32),
            pltpu.VMEM((TILE, table.shape[1]), jnp.float32),
        ],
        compiler_params=pltpu.CompilerParams(vmem_limit_bytes=VMEM_LIMIT),
        cost_estimate=pl.CostEstimate(flops=0, bytes_accessed=40 << 20, transcendentals=0),
        name=f"owner_gather_{chunk}",
    )(asked, table)


def slot_gather_kernel(source, *refs):
    chunks, (out, wide, rows_wide) = refs[:-3], refs[-3:]
    per = chunks[0].shape[0]
    step = 1024

    for k, chunk in enumerate(chunks):

        def widen(i, carry, k=k, chunk=chunk):
            rows = pl.ds(pl.multiple_of(i * step, step), step)
            there = pl.ds(pl.multiple_of(k * per + i * step, step), step)
            wide[there, :] = chunk[rows, :].astype(jnp.float32)
            return carry

        lax.fori_loop(0, per // step, widen, 0)

    def group(i, carry):
        base = pl.multiple_of(i * GATHER_STEP, GATHER_STEP)
        for j in range(GATHER_STEP):
            rows_wide[j : j + 1, :] = wide[pl.ds(source[base + j], 1), :]
        out[pl.ds(base, GATHER_STEP), :] = rows_wide[...].astype(out.dtype)
        return carry

    lax.fori_loop(0, source.shape[0] // GATHER_STEP, group, 0)


def slot_gather(source, chunks):
    width = chunks[0].shape[1]
    return pl.pallas_call(
        slot_gather_kernel,
        out_shape=jax.ShapeDtypeStruct((source.shape[0], width), chunks[0].dtype),
        in_specs=[SMEM] + [VMEM] * len(chunks),
        out_specs=VMEM,
        scratch_shapes=[
            pltpu.VMEM((len(chunks) * chunks[0].shape[0], width), jnp.float32),
            pltpu.VMEM((GATHER_STEP, width), jnp.float32),
        ],
        compiler_params=pltpu.CompilerParams(vmem_limit_bytes=VMEM_LIMIT),
        name="slot_gather",
    )(source, *chunks)


def attention_kernel(
    slice_len, cand_block, live_ref, hist, queries, w_key, w_value, out, keys, values, qt, s_a, s_b
):
    f32, bf16 = jnp.float32, jnp.bfloat16
    requests = live_ref.shape[0]
    blocks = queries.shape[0] // cand_block // requests
    items = blocks * HEADS
    head_dim = keys.shape[1] // HEADS
    scale = 1.0 / math.sqrt(head_dim)
    to_exp2 = scale * math.log2(math.e)
    head_of = lax.broadcasted_iota(jnp.int32, (keys.shape[1], cand_block), 0) // head_dim
    lowest = jnp.full((8, cand_block), -jnp.inf, f32)
    steps = slice_len // ROW_STEP
    proj_step = 1024

    def one_request(r, carry):
        live = live_ref[r]
        for b in range(blocks):
            rows = pl.ds(pl.multiple_of((r * blocks + b) * cand_block, cand_block), cand_block)
            turned = queries[rows, :].astype(f32).T
            for h in range(HEADS):
                qt[b * HEADS + h] = jnp.where(head_of == h, turned, 0.0).astype(bf16)

        def project(i, c):
            rows = pl.ds(pl.multiple_of(i * proj_step, proj_step), proj_step)
            x = hist[pl.ds(pl.multiple_of(r * slice_len + i * proj_step, proj_step), proj_step), :]
            keys[rows, :] = jnp.dot(x, w_key[...], preferred_element_type=f32).astype(bf16)
            turned = lax.dot_general(
                w_value[...], x, (((0,), (1,)), ((), ())), preferred_element_type=f32
            )
            visible = lax.broadcasted_iota(jnp.int32, (1, proj_step), 1) + i * proj_step < live
            turned = jnp.where(visible, turned, 0.0).astype(bf16)
            first = lax.broadcasted_iota(jnp.int32, (16, proj_step), 0) == 0
            ones = jnp.where(first, jnp.where(visible, 1.0, 0.0), 0.0).astype(bf16)
            for h in range(HEADS):
                values[h, 0:head_dim, rows] = turned[h * head_dim : (h + 1) * head_dim]
                values[h, head_dim:HEAD_ROWS, rows] = ones
            return c

        lax.fori_loop(0, slice_len // proj_step, project, 0)

        def score(item, base, peak, scores):
            s = jnp.dot(keys[pl.ds(base, SUB), :], qt[item], preferred_element_type=f32)
            scores[pl.ds(base, SUB), :] = s
            return jnp.maximum(peak, jnp.max(s.reshape(SUB // 8, 8, cand_block), axis=0))

        def first_scores(i, peak):
            for j in range(ROW_STEP // SUB):
                peak = score(0, pl.multiple_of(i * ROW_STEP + j * SUB, SUB), peak, s_a)
            return peak

        def one_item(item, peak, scores, next_scores):
            top = jnp.max(peak, axis=0, keepdims=True)
            h = lax.rem(item, HEADS)
            following = jnp.minimum(item + 1, items - 1)

            def step(i, c):
                next_peak, total = c
                for j in range(ROW_STEP // SUB):
                    base = pl.multiple_of(i * ROW_STEP + j * SUB, SUB)
                    next_peak = score(following, base, next_peak, next_scores)
                    rows = pl.ds(base, SUB)
                    weights = jnp.exp2((scores[rows, :] - top) * to_exp2).astype(bf16)
                    total = total + jnp.dot(
                        values[h, :, rows], weights, preferred_element_type=f32
                    )
                return next_peak, total

            next_peak, total = lax.fori_loop(
                0, steps, step, (lowest, jnp.zeros((HEAD_ROWS, cand_block), f32))
            )
            shown = jnp.where(live > 0, top * scale, NEG_FILL)
            row = lax.broadcasted_iota(jnp.int32, (8, cand_block), 0)
            at = r * blocks + item // HEADS
            out[at, h, 0:head_dim, :] = total[0:head_dim]
            out[at, h, head_dim:PART_ROWS, :] = jnp.where(
                row == 1, shown, total[head_dim:PART_ROWS]
            )
            return next_peak

        def two_items(k, peak):
            peak = one_item(2 * k, peak, s_a, s_b)
            return one_item(2 * k + 1, peak, s_b, s_a)

        lax.fori_loop(0, items // 2, two_items, lax.fori_loop(0, steps, first_scores, lowest))
        return carry

    lax.fori_loop(0, requests, one_request, 0)


def attention(live, hist, queries, w_key, w_value, cand_block):
    requests = live.shape[0]
    slice_len = hist.shape[0] // requests
    width = hist.shape[1]
    blocks = queries.shape[0] // cand_block
    return pl.pallas_call(
        functools.partial(attention_kernel, slice_len, cand_block),
        out_shape=jax.ShapeDtypeStruct((blocks, HEADS, PART_ROWS, cand_block), jnp.float32),
        in_specs=[SMEM] + [VMEM] * 4,
        out_specs=VMEM,
        scratch_shapes=[
            pltpu.VMEM((slice_len, width), jnp.bfloat16),
            pltpu.VMEM((HEADS, HEAD_ROWS, slice_len), jnp.bfloat16),
            pltpu.VMEM((blocks // requests * HEADS, width, cand_block), jnp.bfloat16),
            pltpu.VMEM((slice_len, cand_block), jnp.float32),
            pltpu.VMEM((slice_len, cand_block), jnp.float32),
        ],
        compiler_params=pltpu.CompilerParams(vmem_limit_bytes=VMEM_LIMIT),
        name="attention",
    )(live, hist, queries, w_key, w_value)


def combine_kernel(parts, w_out, out):
    slices = parts.shape[0]
    head_dim = w_out.shape[0] // HEADS
    heads = []
    for h in range(HEADS):
        peaks = [parts[s, h, head_dim + 1 : head_dim + 2, :] for s in range(slices)]
        best = functools.reduce(jnp.maximum, peaks)
        denom = numer = 0.0
        for s in range(slices):
            rescale = jnp.exp(peaks[s] - best)
            denom = denom + rescale * parts[s, h, head_dim : head_dim + 1, :]
            numer = numer + rescale * parts[s, h, 0:head_dim, :]
        heads.append(numer / denom)
    attended = jnp.concatenate(heads, axis=0).T.astype(jnp.bfloat16)
    out[...] = jnp.dot(attended, w_out[...], preferred_element_type=jnp.float32).astype(out.dtype)


def combine(parts, w_out):
    return pl.pallas_call(
        combine_kernel,
        out_shape=jax.ShapeDtypeStruct((parts.shape[3], w_out.shape[1]), jnp.bfloat16),
        in_specs=[VMEM, VMEM],
        out_specs=VMEM,
        name="combine",
    )(parts, w_out)


def shards(
    table,
    fetch_rows,
    tile_counts,
    hist_source,
    cand_source,
    lengths,
    w_query,
    w_key,
    w_value,
    w_out,
):
    del tile_counts
    owners, capacity = fetch_rows.shape[2:]
    tiles = capacity // TILE
    requests, slice_len = hist_source.shape[2:]
    cand_dev = cand_source.shape[2]
    asked = lax.all_to_all(fetch_rows[0, 0], "tbl", split_axis=0, concat_axis=0, tiled=True)
    asked = asked.reshape(-1)
    chunks = []
    for chunk in range(tiles):
        looked = owner_gather(chunk, asked, table, owners)
        there = lax.all_to_all(looked, "tbl", split_axis=0, concat_axis=0, tiled=True)
        chunks.append(there.reshape(owners * TILE, table.shape[1]))

    def place(slot):
        tile = slot % capacity // TILE
        return tile * (owners * TILE) + slot // capacity * TILE + slot % TILE

    live = lengths[0] - lax.axis_index("tm") * slice_len
    source = hist_source[0, 0]
    position = jnp.arange(slice_len, dtype=jnp.int32)[None, :]
    source = jnp.where(position < live[:, None], source, source[:, :1]).reshape(-1)
    source = place(jnp.concatenate((cand_source[0, 0], source)))
    rows = slot_gather(source, chunks)
    own_cands, hist = rows[:cand_dev], rows[cand_dev:]
    cands = lax.all_gather(own_cands, "tm", axis=0, tiled=True)
    queries = jnp.dot(cands, w_query, preferred_element_type=jnp.float32).astype(jnp.bfloat16)
    parts = attention(live, hist, queries, w_key, w_value, cand_dev)
    parts = lax.all_to_all(parts, "tm", split_axis=0, concat_axis=0, tiled=True)
    return combine(parts, w_out)


def solution(mesh):
    return jax.shard_map(
        shards,
        mesh=mesh,
        in_specs=(
            P("tbl", None),
            P("tbl", "tm", None, None),
            P("tbl", "tm", None),
            P("tbl", "tm", None, None),
            P("tbl", "tm", None),
            P("tbl", None),
            P(),
            P(),
            P(),
            P(),
        ),
        out_specs=P(("tbl", "tm"), None),
        check_vma=False,
    )
```

time: 881 us -> 396 us (0.45)
  local copies, waits for them, and re-layouts: 258 us -> 5.07 us
  matrix products: 219 us -> 1.11 us
  Pallas kernels: 0 us -> 148 us
  other arithmetic: 110 us -> 0.89 us
  waiting for transfers between devices: 210 us -> 160 us
  starting transfers between devices: 6.68 us -> 24.8 us
  between operations: 13.7 us -> 0.13 us
    dot_general x35 -> x1, matrix products: 219 us -> 1.11 us  [shards(): jnp.dot(cands, w_query, preferred_element_type=jnp.float32)]
    gather x3 -> x0, local copies, waits for them, and re-layouts: 180 us -> none  [the longest x1 115 us: shards(): jnp.take(table, lax.all_to_all(tile_ids, 'tbl', split_axis=0, concat_axis...]
    pallas_call x0 -> x7, Pallas kernels: none -> 148 us  [the longest x1 70.5 us: attention(): pl.pallas_call(functools.partial(attention_kernel, slice_len, cand_block)...]
    reduce_sum x16 -> x0, other arithmetic: 83.2 us -> none  [one_block(): weight_sum = jnp.sum(weights, axis=2, dtype=jnp.float32)]
    all_to_all x1 -> x4, waiting for transfers between devices: 186 us -> 160 us  [shards(): lax.all_to_all(looked, 'tbl', split_axis=0, concat_axis=0, tiled=True)]
    all_gather x3 -> x1, blocking collectives: 37.9 us -> 13.1 us  [shards(): cands = lax.all_gather(own_cands, 'tm', axis=0, tiled=True)]
    all_gather x1 -> x0, waiting for transfers between devices: 24.3 us -> none  [joined(): everything = jax.tree.map(lambda part: lax.all_gather(part, axis), array)]
    while x35 -> x0, local copies, waits for them, and re-layouts: 22.7 us -> none  [the longest x2 13.7 us: shards(): lax.map(one_request, (queries, keys_all, values_all, live_all))]
  transfers between devices with their start and end apart: 2 -> 4, of which waited for: 2 -> 4; matrix products, arithmetic and copies ran while one was open for 0% -> 0% of each run, Pallas kernels for 0% -> 10%
where the time goes in v1:
time: 396 us; the launch traced here: 395 us
  waiting for transfers between devices  160 us (40%)
  Pallas kernels  148 us (37%)
  blocking collectives  55.8 us (14%)
  starting transfers between devices  24.8 us (6%)
  local copies, waits for them, and re-layouts  5.07 us (1%)
    all_to_all x4, waiting for transfers between devices, shards(): lax.all_to_all(looked, 'tbl', split_axis=0, concat_axis=0, tiled=True)  160 us
    pallas_call x1, Pallas kernels, attention(): pl.pallas_call(functools.partial(attention_kernel, slice_len, cand_block)...  70.5 us
    pallas_call x4, Pallas kernels, owner_gather(): pl.pallas_call(functools.partial(owner_gather_kernel, chunk), out_shape=j...  54 us
    all_to_all x4, starting transfers between devices, shards(): lax.all_to_all(looked, 'tbl', split_axis=0, concat_axis=0, tiled=True)  24.8 us
    all_to_all x1, blocking collectives, shards(): lax.all_to_all(fetch_rows[0, 0], 'tbl', split_axis=0, concat_axis=0, tile...  21.8 us
    pallas_call x1, Pallas kernels, slot_gather(): pl.pallas_call(slot_gather_kernel, out_shape=jax.ShapeDtypeStruct((source...  21.2 us
    all_to_all x1, blocking collectives, shards(): parts = lax.all_to_all(parts, 'tm', split_axis=0, concat_axis=0, tiled=True)  20.8 us
    all_gather x1, blocking collectives, shards(): cands = lax.all_gather(own_cands, 'tm', axis=0, tiled=True)  13.1 us
  transfers between devices with their start and end apart: 4, of which 4 were waited for; matrix products, arithmetic and copies ran while one was open for 0% of the time, Pallas kernels for 10%

profile of v1, /device:TPU:32, one launch (start us, length us, event | category | flops | bytes accessed | tf_op | source)
XLA Modules:
  0.0 395.4 jit_solution(2165650759665912358)
XLA Ops:
  0.0 1.0 all_to_all.21
  1.0 21.8 %all_to_all.34 = s32[64,1,512]{2,1,0:T(1,128)} all-to-all(s32[64,1,512]{2,1,0:T(1,128)S(1)} %all_to_all.21), channel_id=1, replica_groups=mesh['tbl'=64,'tm'=4] {'tbl'}, dimensions={0} | all-to-all | bytes 262144 | tf_op jit(solution)/shard_map/all_to_all | solution.py:259
  22.9 13.5 %owner_gather_3.1 = bf16[64,128,128]{2,1,0:T(8,128)(2,1)} custom-call(s32[32768]{0:T(1024)} %bitcast.20, bf16[32768,128]{1,0:T(8,128)(2,1)} %table.7), custom_call_target="tpu_custom_call" | custom-call | bytes 41943040 | tf_op jit(solution)/shard_map/owner_gather_3/pallas_call | solution.py:47
  36.3 5.5 %all-to-all-start.4 = ((bf16[64,128,128]{2,1,0:T(8,128)(2,1)}), bf16[64,128,128]{2,1,0:T(8,128)(2,1)S(1)}, u32[]{:S(2)}, u32[]{:S(2)}) async-start(bf16[64,128,128]{2,1,0:T(8,128)(2,1)} %owner_gather_3.1), calls=%async_computation.4 | async-start | bytes 4194304 | tf_op jit(solution)/shard_map/all_to_all | solution.py:264
  41.8 13.5 %owner_gather_2.1 = bf16[64,128,128]{2,1,0:T(8,128)(2,1)} custom-call(s32[32768]{0:T(1024)} %bitcast.21, bf16[32768,128]{1,0:T(8,128)(2,1)} %table.7), custom_call_target="tpu_custom_call" | custom-call | bytes 41943040 | tf_op jit(solution)/shard_map/owner_gather_2/pallas_call | solution.py:47
  55.3 37.0 %all-to-all-done.4 = bf16[64,128,128]{2,1,0:T(8,128)(2,1)S(1)} async-done(((bf16[64,128,128]{2,1,0:T(8,128)(2,1)}), bf16[64,128,128]{2,1,0:T(8,128)(2,1)S(1)}, u32[]{:S(2)}, u32[]{:S(2)}) %all-to-all-start.4) | async-done | bytes 2097184 | tf_op jit(solution)/shard_map/all_to_all | solution.py:264
  92.3 6.5 %all-to-all-start.3 = ((bf16[64,128,128]{2,1,0:T(8,128)(2,1)}), bf16[64,128,128]{2,1,0:T(8,128)(2,1)}, u32[]{:S(2)}, u32[]{:S(2)}) async-start(bf16[64,128,128]{2,1,0:T(8,128)(2,1)} %owner_gather_2.1), calls=%async_computation.3 | async-start | bytes 4194304 | tf_op jit(solution)/shard_map/all_to_all | solution.py:264
  98.8 13.5 %owner_gather_1.1 = bf16[64,128,128]{2,1,0:T(8,128)(2,1)} custom-call(s32[32768]{0:T(1024)} %bitcast.22, bf16[32768,128]{1,0:T(8,128)(2,1)} %table.7), custom_call_target="tpu_custom_call" | custom-call | bytes 41943040 | tf_op jit(solution)/shard_map/owner_gather_1/pallas_call | solution.py:47
  112.2 36.9 %all-to-all-done.3 = bf16[64,128,128]{2,1,0:T(8,128)(2,1)} async-done(((bf16[64,128,128]{2,1,0:T(8,128)(2,1)}), bf16[64,128,128]{2,1,0:T(8,128)(2,1)}, u32[]{:S(2)}, u32[]{:S(2)}) %all-to-all-start.3) | async-done | bytes 2097184 | tf_op jit(solution)/shard_map/all_to_all | solution.py:264
  149.1 6.3 %all-to-all-start.2 = ((bf16[64,128,128]{2,1,0:T(8,128)(2,1)}), bf16[64,128,128]{2,1,0:T(8,128)(2,1)S(1)}, u32[]{:S(2)}, u32[]{:S(2)}) async-start(bf16[64,128,128]{2,1,0:T(8,128)(2,1)} %owner_gather_1.1), calls=%async_computation.2 | async-start | bytes 4194304 | tf_op jit(solution)/shard_map/all_to_all | solution.py:264
  155.4 13.6 %owner_gather_0.1 = bf16[64,128,128]{2,1,0:T(8,128)(2,1)} custom-call(s32[32768]{0:T(1024)} %bitcast.23, bf16[32768,128]{1,0:T(8,128)(2,1)} %table.7), custom_call_target="tpu_custom_call" | custom-call | bytes 41943040 | tf_op jit(solution)/shard_map/owner_gather_0/pallas_call | solution.py:47
  169.0 36.8 %all-to-all-done.2 = bf16[64,128,128]{2,1,0:T(8,128)(2,1)S(1)} async-done(((bf16[64,128,128]{2,1,0:T(8,128)(2,1)}), bf16[64,128,128]{2,1,0:T(8,128)(2,1)S(1)}, u32[]{:S(2)}, u32[]{:S(2)}) %all-to-all-start.2) | async-done | bytes 2097184 | tf_op jit(solution)/shard_map/all_to_all | solution.py:264
  205.8 6.5 %all-to-all-start.1 = ((bf16[64,128,128]{2,1,0:T(8,128)(2,1)}), bf16[64,128,128]{2,1,0:T(8,128)(2,1)}, u32[]{:S(2)}, u32[]{:S(2)}) async-start(bf16[64,128,128]{2,1,0:T(8,128)(2,1)} %owner_gather_0.1), calls=%async_computation.1 | async-start | bytes 4194304 | tf_op jit(solution)/shard_map/all_to_all | solution.py:264
  212.3 0.1 iota_compare_fusion
  212.5 0.1 slice_reduce_fusion
  212.8 0.8 fusion.3.source
  213.6 49.1 %all-to-all-done.1 = bf16[64,128,128]{2,1,0:T(8,128)(2,1)} async-done(((bf16[64,128,128]{2,1,0:T(8,128)(2,1)}), bf16[64,128,128]{2,1,0:T(8,128)(2,1)}, u32[]{:S(2)}, u32[]{:S(2)}) %all-to-all-start.1) | async-done | bytes 2097184 | tf_op jit(solution)/shard_map/all_to_all | solution.py:264
  262.6 21.2 %slot_gather.1 = bf16[16896,128]{1,0:T(8,128)(2,1)} custom-call(s32[16896]{0:T(1024)} %fusion.3.source, bf16[8192,128]{1,0:T(8,128)(2,1)} %bitcast.4.refs_0_, bf16[8192,128]{1,0:T(8,128)(2,1)} %bitcast.19, bf16[8192,128]{1,0:T(8,128)(2,1)} %bitcast.6.refs_2_, bf16[8192,128]{1,0:T(8,128)(2,1)} %bitcast.18), custom_call_target="tpu_custom_call" | custom-call | tf_op jit(solution)/shard_map/slot_gather/pallas_call | solution.py:89
  283.8 3.8 slice.13.hist
  287.6 13.1 %all_gather.3 = bf16[2048,128]{1,0:T(8,128)(2,1)S(1)} all-gather(bf16[512,128]{1,0:T(8,128)(2,1)S(1)} %slice-done), channel_id=1, replica_groups=mesh['tbl'=64,'tm'=4] {'tm'}, dimensions={0}, use_global_device_ids=true | all-gather | bytes 655360 | tf_op jit(solution)/shard_map/all_gather | solution.py:278
  300.7 1.1 convolution_convert_fusion.queries
  301.8 70.5 %attention.1 = f32[4,4,40,512]{3,2,1,0:T(8,128)} custom-call(s32[2]{0:T(128)} %copy-done.5, bf16[16384,128]{1,0:T(8,128)(2,1)} %slice.13.hist, bf16[2048,128]{1,0:T(8,128)(2,1)} %convolution_convert_fusion.queries, bf16[128,128]{1,0:T(8,128)(2,1)} %w_key.1, bf16[128,128]{1,0:T(8,128)(2,1)} %w_value.1), custom_call_target="tpu_custom_call" | custom-call | tf_op jit(solution)/shard_map/attention/pallas_call | solution.py:198
  372.3 20.8 %all_to_all.35.parts = f32[4,4,40,512]{3,2,1,0:T(8,128)} all-to-all(f32[4,4,40,512]{3,2,1,0:T(8,128)} %attention.1), channel_id=1, replica_groups=mesh['tbl'=64,'tm'=4] {'tm'}, dimensions={0} | all-to-all | bytes 2621440 | tf_op jit(solution)/shard_map/all_to_all | solution.py:281
  393.1 2.3 combine.1
  (22 shorter events, 0.2 us)
Async XLA Ops:
  0.0 300.7 %copy-start = (bf16[128,128]{1,0:T(8,128)(2,1)S(1)}, bf16[128,128]{1,0:T(8,128)(2,1)}, u32[]{:S(2)}) copy-start(bf16[128,128]{1,0:T(8,128)(2,1)} %param.15) | copy-start | bytes 98308
  36.3 56.0 %all-to-all-start.4 = ((bf16[64,128,128]{2,1,0:T(8,128)(2,1)}), bf16[64,128,128]{2,1,0:T(8,128)(2,1)S(1)}, u32[]{:S(2)}, u32[]{:S(2)}) async-start(bf16[64,128,128]{2,1,0:T(8,128)(2,1)} %owner_gather_3.1), calls=%async_computation.4 | async-start | bytes 4194304 | tf_op jit(solution)/shard_map/all_to_all | solution.py:264
  92.3 20.0 %copy-start.1 = (bf16[64,128,128]{2,1,0:T(8,128)(2,1)}, bf16[64,128,128]{2,1,0:T(8,128)(2,1)S(1)}, u32[]{:S(2)}) copy-start(bf16[64,128,128]{2,1,0:T(8,128)(2,1)S(1)} %all-to-all-done.4) | copy-start | bytes 6291460
  92.3 56.8 %all-to-all-start.3 = ((bf16[64,128,128]{2,1,0:T(8,128)(2,1)}), bf16[64,128,128]{2,1,0:T(8,128)(2,1)}, u32[]{:S(2)}, u32[]{:S(2)}) async-start(bf16[64,128,128]{2,1,0:T(8,128)(2,1)} %owner_gather_2.1), calls=%async_computation.3 | async-start | bytes 4194304 | tf_op jit(solution)/shard_map/all_to_all | solution.py:264
  149.1 56.7 %all-to-all-start.2 = ((bf16[64,128,128]{2,1,0:T(8,128)(2,1)}), bf16[64,128,128]{2,1,0:T(8,128)(2,1)S(1)}, u32[]{:S(2)}, u32[]{:S(2)}) async-start(bf16[64,128,128]{2,1,0:T(8,128)(2,1)} %owner_gather_1.1), calls=%async_computation.2 | async-start | bytes 4194304 | tf_op jit(solution)/shard_map/all_to_all | solution.py:264
  169.0 43.3 %copy-start.6 = (s32[1,2]{1,0:T(1,128)S(1)}, s32[1,2]{1,0:T(1,128)}, u32[]{:S(2)}) copy-start(s32[1,2]{1,0:T(1,128)} %param.14) | copy-start | bytes 28
  169.0 43.5 %copy-start.3 = (s32[1,1,2,8192]{3,2,1,0:T(2,128)S(1)}, s32[1,1,2,8192]{3,2,1,0:T(2,128)}, u32[]{:S(2)}) copy-start(s32[1,1,2,8192]{3,2,1,0:T(2,128)} %param.12) | copy-start | bytes 196612
  169.0 43.7 %copy-start.4 = (s32[1,1,512]{2,1,0:T(1,128)S(1)}, s32[1,1,512]{2,1,0:T(1,128)}, u32[]{:S(2)}) copy-start(s32[1,1,512]{2,1,0:T(1,128)} %param.13) | copy-start | bytes 6148
  205.8 6.5 %copy-start.2 = (bf16[64,128,128]{2,1,0:T(8,128)(2,1)}, bf16[64,128,128]{2,1,0:T(8,128)(2,1)S(1)}, u32[]{:S(2)}) copy-start(bf16[64,128,128]{2,1,0:T(8,128)(2,1)S(1)} %all-to-all-done.2) | copy-start | bytes 6291460
  205.8 56.8 %all-to-all-start.1 = ((bf16[64,128,128]{2,1,0:T(8,128)(2,1)}), bf16[64,128,128]{2,1,0:T(8,128)(2,1)}, u32[]{:S(2)}, u32[]{:S(2)}) async-start(bf16[64,128,128]{2,1,0:T(8,128)(2,1)} %owner_gather_0.1), calls=%async_computation.1 | async-start | bytes 4194304 | tf_op jit(solution)/shard_map/all_to_all | solution.py:264
  212.3 71.5 %copy-start.5 = (s32[2]{0:T(128)}, s32[2]{0:T(128)S(1)}, u32[]{:S(2)}) copy-start(s32[2]{0:T(128)S(1)} %subtract_bitcast_fusion.live_ref) | copy-start | bytes 28
  283.8 3.8 slice-start

commit v2 on v1

v2 whole, which is shorter than its diff:
```python
import functools
import math

import jax
import jax.numpy as jnp
from jax import lax
from jax.experimental import pallas as pl
from jax.experimental.pallas import tpu as pltpu
from jax.sharding import PartitionSpec as P

HEADS = 4
TILE = 128
CAND_DEV = 512
HEAD_ROWS = 48
PART_ROWS = 40
ROW_STEP = 2048
SUB = 256
GATHER_STEP = 256
VMEM_LIMIT = 58 << 20
NEG_FILL = -1e30

VMEM = pl.BlockSpec(memory_space=pltpu.VMEM)
SMEM = pl.BlockSpec(memory_space=pltpu.SMEM)
MESH = pl.DeviceIdType.MESH
STRIDE = 27


def fetch_kernel(
    devices,
    ids,
    table,
    out,
    wide,
    landing,
    asked,
    rows_wide,
    found,
    ids_send,
    ids_recv,
    row_send,
    row_recv,
    own_sem,
):
    me = lax.axis_index("tbl")
    capacity = found.shape[1]

    def forward(k):
        return lax.rem(me + k * STRIDE, devices)

    barrier = pltpu.get_barrier_semaphore()

    def greet(k, carry):
        pl.semaphore_signal(barrier, 1, device_id={"tbl": forward(k)}, device_id_type=MESH)
        return carry

    lax.fori_loop(1, devices, greet, 0)
    pl.semaphore_wait(barrier, devices - 1)

    def ids_copy(k):
        peer = forward(k)
        return pltpu.make_async_remote_copy(
            src_ref=ids.at[peer],
            dst_ref=landing.at[me],
            send_sem=ids_send.at[k],
            recv_sem=ids_recv.at[k],
            device_id={"tbl": peer},
            device_id_type=MESH,
        )

    def send_ids(k, carry):
        ids_copy(k).start()
        return carry

    lax.fori_loop(1, devices, send_ids, 0)
    landing[me] = ids[me]
    step = 1024

    def widen(i, carry):
        rows = pl.ds(pl.multiple_of(i * step, step), step)
        wide[rows, :] = table[rows, :].astype(jnp.float32)
        return carry

    lax.fori_loop(0, table.shape[0] // step, widen, 0)

    def wait_ids(k, carry):
        ids_copy(k).wait()
        return carry

    lax.fori_loop(1, devices, wait_ids, 0)
    listed = pltpu.make_async_copy(landing, asked, own_sem)
    listed.start()
    listed.wait()

    def look_up(k):
        peer = forward(k)

        def group(i, carry):
            for j in range(GATHER_STEP):
                row = asked[peer, i * (GATHER_STEP // TILE) + j // TILE, j % TILE]
                rows_wide[j : j + 1, :] = wide[pl.ds(row, 1), :]
            rows = pl.ds(pl.multiple_of(i * GATHER_STEP, GATHER_STEP), GATHER_STEP)
            found[k, rows, :] = rows_wide[...].astype(found.dtype)
            return carry

        lax.fori_loop(0, capacity // GATHER_STEP, group, 0)

    def row_copy(k):
        return pltpu.make_async_remote_copy(
            src_ref=found.at[k],
            dst_ref=out.at[me],
            send_sem=row_send.at[k],
            recv_sem=row_recv.at[k],
            device_id={"tbl": forward(k)},
            device_id_type=MESH,
        )

    def send_rows(k, carry):
        look_up(k)
        row_copy(k).start()
        return carry

    lax.fori_loop(1, devices, send_rows, 0)
    look_up(0)
    own = pltpu.make_async_copy(found.at[0], out.at[me], own_sem)
    own.start()

    def wait_rows(k, carry):
        row_copy(k).wait()
        return carry

    lax.fori_loop(1, devices, wait_rows, 0)
    own.wait()


def fetch(ids, table):
    devices, capacity = ids.shape
    width = table.shape[1]
    tiles = capacity // TILE
    return pl.pallas_call(
        functools.partial(fetch_kernel, devices),
        out_shape=jax.ShapeDtypeStruct((devices, capacity, width), table.dtype),
        in_specs=[VMEM, VMEM],
        out_specs=pl.BlockSpec(memory_space=pl.ANY),
        scratch_shapes=[
            pltpu.VMEM(table.shape, jnp.float32),
            pltpu.VMEM((devices, tiles, TILE), jnp.int32),
            pltpu.SMEM((devices, tiles, TILE), jnp.int32),
            pltpu.VMEM((GATHER_STEP, width), jnp.float32),
            pltpu.VMEM((devices, capacity, width), table.dtype),
        ]
        + [pltpu.SemaphoreType.DMA((devices,))] * 4
        + [pltpu.SemaphoreType.DMA],
        compiler_params=pltpu.CompilerParams(
            collective_id=1, has_side_effects=True, vmem_limit_bytes=VMEM_LIMIT
        ),
        name="fetch",
    )(ids.reshape(devices, tiles, TILE), table)


def attend_kernel(
    live_ref,
    source,
    fetched,
    w_query,
    w_key,
    w_value,
    w_out,
    out,
    wide,
    scores_b,
    rows_wide,
    cands,
    hist,
    keys,
    values,
    qt,
    parts,
    arrived,
    cand_send,
    cand_recv,
    part_send,
    part_recv,
):
    f32, bf16 = jnp.float32, jnp.bfloat16
    slices, cand_block = cands.shape[:2]
    requests = live_ref.shape[0]
    width = keys.shape[1]
    slice_len = keys.shape[0]
    blocks = slices // requests
    items = blocks * HEADS
    head_dim = width // HEADS
    scale = 1.0 / math.sqrt(head_dim)
    to_exp2 = scale * math.log2(math.e)
    me = lax.axis_index("tm")

    barrier = pltpu.get_barrier_semaphore()
    for off in range(1, slices):
        pl.semaphore_signal(
            barrier, 1, device_id={"tm": lax.rem(me + off, slices)}, device_id_type=MESH
        )
    pl.semaphore_wait(barrier, slices - 1)

    step = 1024

    def widen(i, carry):
        rows = pl.ds(pl.multiple_of(i * step, step), step)
        wide[rows, :] = fetched[rows, :].astype(f32)
        return carry

    lax.fori_loop(0, fetched.shape[0] // step, widen, 0)

    def gather(first):
        for j in range(GATHER_STEP):
            rows_wide[j : j + 1, :] = wide[pl.ds(source[first + j], 1), :]
        return rows_wide[...].astype(bf16)

    def cand_group(i, carry):
        base = pl.multiple_of(i * GATHER_STEP, GATHER_STEP)
        cands[me, pl.ds(base, GATHER_STEP), :] = gather(base)
        return carry

    lax.fori_loop(0, cand_block // GATHER_STEP, cand_group, 0)

    def cand_copy(off):
        return pltpu.make_async_remote_copy(
            src_ref=cands.at[me],
            dst_ref=cands.at[me],
            send_sem=cand_send.at[off],
            recv_sem=cand_recv.at[off],
            device_id={"tm": lax.rem(me + off, slices)},
            device_id_type=MESH,
        )

    for off in range(1, slices):
        cand_copy(off).start()

    def hist_group(i, carry):
        base = pl.multiple_of(i * GATHER_STEP, GATHER_STEP)
        hist[pl.ds(base, GATHER_STEP), :] = gather(cand_block + base)
        return carry

    lax.fori_loop(0, requests * slice_len // GATHER_STEP, hist_group, 0)
    for off in range(1, slices):
        cand_copy(off).wait()

    def part_copy(off, h):
        there = lax.rem(me + off, slices)
        return pltpu.make_async_remote_copy(
            src_ref=parts.at[there, h],
            dst_ref=arrived.at[me, h],
            send_sem=part_send.at[off, h],
            recv_sem=part_recv.at[off, h],
            device_id={"tm": there},
            device_id_type=MESH,
        )

    head_of = lax.broadcasted_iota(jnp.int32, (width, cand_block), 0) // head_dim
    lowest = jnp.full((8, cand_block), -jnp.inf, f32)
    steps = slice_len // ROW_STEP
    lanes = cand_block // TILE

    def put_a(base, s):
        for c in range(lanes):
            wide[pl.ds(c * slice_len + base, SUB), :] = s[:, c * TILE : (c + 1) * TILE]

    def get_a(base):
        return jnp.concatenate(
            [wide[pl.ds(c * slice_len + base, SUB), :] for c in range(lanes)], axis=1
        )

    def put_b(base, s):
        scores_b[pl.ds(base, SUB), :] = s

    def get_b(base):
        return scores_b[pl.ds(base, SUB), :]

    def one_request(turn, carry):
        r = lax.rem(me // blocks + 1 + turn, requests)
        live = live_ref[r]

        def block_of(j):
            return r * blocks + lax.rem(me + 1 + j, blocks)

        for b in range(blocks):
            query = jnp.dot(cands[block_of(b)], w_query[...], preferred_element_type=f32)
            turned = query.astype(bf16).astype(f32).T
            for h in range(HEADS):
                qt[b * HEADS + h] = jnp.where(head_of == h, turned, 0.0).astype(bf16)

        def project(i, c):
            rows = pl.ds(pl.multiple_of(i * step, step), step)
            x = hist[pl.ds(pl.multiple_of(r * slice_len + i * step, step), step), :]
            keys[rows, :] = jnp.dot(x, w_key[...], preferred_element_type=f32).astype(bf16)
            turned = lax.dot_general(
                w_value[...], x, (((0,), (1,)), ((), ())), preferred_element_type=f32
            )
            visible = lax.broadcasted_iota(jnp.int32, (1, step), 1) + i * step < live
            turned = jnp.where(visible, turned, 0.0).astype(bf16)
            first = lax.broadcasted_iota(jnp.int32, (16, step), 0) == 0
            ones = jnp.where(first, jnp.where(visible, 1.0, 0.0), 0.0).astype(bf16)
            for h in range(HEADS):
                values[h, 0:head_dim, rows] = turned[h * head_dim : (h + 1) * head_dim]
                values[h, head_dim:HEAD_ROWS, rows] = ones
            return c

        lax.fori_loop(0, slice_len // step, project, 0)

        def score(item, base, peak, put):
            s = jnp.dot(keys[pl.ds(base, SUB), :], qt[item], preferred_element_type=f32)
            put(base, s)
            return jnp.maximum(peak, jnp.max(s.reshape(SUB // 8, 8, cand_block), axis=0))

        def first_scores(i, peak):
            for j in range(ROW_STEP // SUB):
                peak = score(0, pl.multiple_of(i * ROW_STEP + j * SUB, SUB), peak, put_a)
            return peak

        def one_item(item, peak, get, put_next):
            top = jnp.max(peak, axis=0, keepdims=True)
            h = lax.rem(item, HEADS)
            following = jnp.minimum(item + 1, items - 1)

            def attend_step(i, c):
                next_peak, total = c
                for j in range(ROW_STEP // SUB):
                    base = pl.multiple_of(i * ROW_STEP + j * SUB, SUB)
                    next_peak = score(following, base, next_peak, put_next)
                    weights = jnp.exp2((get(base) - top) * to_exp2).astype(bf16)
                    total = total + jnp.dot(
                        values[h, :, pl.ds(base, SUB)], weights, preferred_element_type=f32
                    )
                return next_peak, total

            next_peak, total = lax.fori_loop(
                0, steps, attend_step, (lowest, jnp.zeros((HEAD_ROWS, cand_block), f32))
            )
            shown = jnp.where(live > 0, top * scale, NEG_FILL)
            row = lax.broadcasted_iota(jnp.int32, (8, cand_block), 0)
            tail = jnp.where(row == 1, shown, total[head_dim:PART_ROWS])
            there = block_of(item // HEADS)

            @pl.when(there != me)
            def _():
                parts[there, h, 0:head_dim, :] = total[0:head_dim]
                parts[there, h, head_dim:PART_ROWS, :] = tail
                part_copy(lax.rem(there - me + slices, slices), h).start()

            @pl.when(there == me)
            def _():
                arrived[me, h, 0:head_dim, :] = total[0:head_dim]
                arrived[me, h, head_dim:PART_ROWS, :] = tail

            return next_peak

        def two_items(k, peak):
            peak = one_item(2 * k, peak, get_a, put_b)
            return one_item(2 * k + 1, peak, get_b, put_a)

        lax.fori_loop(0, items // 2, two_items, lax.fori_loop(0, steps, first_scores, lowest))
        return carry

    lax.fori_loop(0, requests, one_request, 0)
    for off in range(1, slices):
        for h in range(HEADS):
            part_copy(off, h).wait()

    heads = []
    for h in range(HEADS):
        peaks = [arrived[s, h, head_dim + 1 : head_dim + 2, :] for s in range(slices)]
        best = functools.reduce(jnp.maximum, peaks)
        denom = numer = 0.0
        for s in range(slices):
            rescale = jnp.exp(peaks[s] - best)
            denom = denom + rescale * arrived[s, h, head_dim : head_dim + 1, :]
            numer = numer + rescale * arrived[s, h, 0:head_dim, :]
        heads.append(numer / denom)
    attended = jnp.concatenate(heads, axis=0).T.astype(bf16)
    out[...] = jnp.dot(attended, w_out[...], preferred_element_type=f32).astype(out.dtype)


def attend(live, source, fetched, w_query, w_key, w_value, w_out, slices):
    requests = live.shape[0]
    width = fetched.shape[1]
    cand_block = CAND_DEV
    slice_len = (source.shape[0] - cand_block) // requests
    bf16, f32 = jnp.bfloat16, jnp.float32
    part = (slices, HEADS, PART_ROWS, cand_block)
    return pl.pallas_call(
        attend_kernel,
        out_shape=jax.ShapeDtypeStruct((cand_block, w_out.shape[1]), bf16),
        in_specs=[SMEM, SMEM] + [VMEM] * 5,
        out_specs=VMEM,
        scratch_shapes=[
            pltpu.VMEM(fetched.shape, f32),
            pltpu.VMEM((slice_len, cand_block), f32),
            pltpu.VMEM((GATHER_STEP, width), f32),
            pltpu.VMEM((slices, cand_block, width), bf16),
            pltpu.VMEM((requests * slice_len, width), bf16),
            pltpu.VMEM((slice_len, width), bf16),
            pltpu.VMEM((HEADS, HEAD_ROWS, slice_len), bf16),
            pltpu.VMEM((slices // requests * HEADS, width, cand_block), bf16),
            pltpu.VMEM(part, f32),
            pltpu.VMEM(part, f32),
            pltpu.SemaphoreType.DMA((slices,)),
            pltpu.SemaphoreType.DMA((slices,)),
            pltpu.SemaphoreType.DMA((slices, HEADS)),
            pltpu.SemaphoreType.DMA((slices, HEADS)),
        ],
        compiler_params=pltpu.CompilerParams(
            collective_id=2, has_side_effects=True, vmem_limit_bytes=VMEM_LIMIT
        ),
        name="attend",
    )(live, source, fetched, w_query, w_key, w_value, w_out)


def shards(
    table,
    fetch_rows,
    tile_counts,
    hist_source,
    cand_source,
    lengths,
    w_query,
    w_key,
    w_value,
    w_out,
):
    del tile_counts
    requests, slice_len = hist_source.shape[2:]
    fetched = fetch(fetch_rows[0, 0], table).reshape(-1, table.shape[1])
    live = lengths[0] - lax.axis_index("tm") * slice_len
    source = hist_source[0, 0]
    position = jnp.arange(slice_len, dtype=jnp.int32)[None, :]
    source = jnp.where(position < live[:, None], source, source[:, :1]).reshape(-1)
    source = jnp.concatenate((cand_source[0, 0], source))
    slices = lax.axis_size("tm")
    return attend(live, source, fetched, w_query, w_key, w_value, w_out, slices)


def solution(mesh):
    return jax.shard_map(
        shards,
        mesh=mesh,
        in_specs=(
            P("tbl", None),
            P("tbl", "tm", None, None),
            P("tbl", "tm", None),
            P("tbl", "tm", None, None),
            P("tbl", "tm", None),
            P("tbl", None),
            P(),
            P(),
            P(),
            P(),
        ),
        out_specs=P(("tbl", "tm"), None),
        check_vma=False,
    )
```

time: 396 us -> 309 us (0.78)
  waiting for transfers between devices: 160 us -> 0 us
  Pallas kernels: 148 us -> 302 us
  blocking collectives: 55.8 us -> 0 us
  starting transfers between devices: 24.8 us -> 0 us
    all_to_all x4 -> x0, waiting for transfers between devices: 160 us -> none  [shards(): lax.all_to_all(looked, 'tbl', split_axis=0, concat_axis=0, tiled=True)]
    pallas_call x7 -> x2, Pallas kernels: 148 us -> 302 us  [the longest x1 210 us: fetch(): pl.pallas_call(functools.partial(fetch_kernel, devices), out_shape=jax.Sh...]
    all_to_all x2 -> x0, blocking collectives: 42.7 us -> none  [the longest x1 21.8 us: shards(): lax.all_to_all(fetch_rows[0, 0], 'tbl', split_axis=0, concat_axis=0, tile...]
    all_to_all x4 -> x0, starting transfers between devices: 24.8 us -> none  [shards(): lax.all_to_all(looked, 'tbl', split_axis=0, concat_axis=0, tiled=True)]
    all_gather x1 -> x0, blocking collectives: 13.1 us -> none  [shards(): cands = lax.all_gather(own_cands, 'tm', axis=0, tiled=True)]
  transfers between devices with their start and end apart: 4 -> 0, of which waited for: 4 -> 0; matrix products, arithmetic and copies ran while one was open for 0% -> 0% of each run, Pallas kernels for 10% -> 0%
where the time goes in v2:
time: 309 us
  Pallas kernels  302 us (98%)
  local copies, waits for them, and re-layouts  4.97 us (2%)
    pallas_call x1, Pallas kernels, fetch(): pl.pallas_call(functools.partial(fetch_kernel, devices), out_shape=jax.Sh...  210 us
    pallas_call x1, Pallas kernels, attend(): pl.pallas_call(attend_kernel, out_shape=jax.ShapeDtypeStruct((cand_block,...  91.4 us

profile of v2, /device:TPU:32, one launch (start us, length us, event | category | flops | bytes accessed | tf_op | source)
XLA Modules:
  0.0 309.0 jit_solution(4086327953193834304)
XLA Ops:
  0.0 0.7 subtract_bitcast_fusion.live_ref
  0.7 0.0 copy-start
  0.7 0.8 slice_reduce_fusion
  1.5 0.1 iota_compare_fusion
  1.6 0.1 lt.20
  1.6 0.1 broadcast_bitcast_fusion
  1.7 0.8 copy.10
  2.6 1.3 pad_add_fusion.source
  3.9 1.6 reshape_squeeze.3.ids
  5.5 210.5 %fetch.1 = bf16[64,512,128]{2,1,0:T(8,128)(2,1)} custom-call(s32[64,4,128]{2,1,0:T(4,128)} %reshape_squeeze.3.ids, bf16[32768,128]{1,0:T(8,128)(2,1)} %table.1), custom_call_target="tpu_custom_call" | custom-call | tf_op jit(solution)/shard_map/fetch/pallas_call | solution.py:139
  216.0 0.0 copy-done
  216.0 91.4 %attend.1 = bf16[512,128]{1,0:T(8,128)(2,1)} custom-call(s32[2]{0:T(128)} %copy-done, s32[16896]{0:T(1024)} %pad_add_fusion.source, bf16[32768,128]{1,0:T(8,128)(2,1)} %bitcast.12, bf16[128,128]{1,0:T(8,128)(2,1)} %w_query.1, bf16[128,128]{1,0:T(8,128)(2,1)} %w_key.1, bf16[128,128]{1,0:T(8,128)(2,1)} %w_value.1, bf16[128,128]{1,0:T(8,128)(2,1)} %w_out.1), custom_call_target="tpu_custom_call" | custom-call | tf_op jit(solution)/shard_map/attend/pallas_call | solution.py:388
  307.4 1.6 copy.13
  (2 shorter events, 0.0 us)
Async XLA Ops:
  0.7 215.3 %copy-start = (s32[2]{0:T(128)}, s32[2]{0:T(128)S(1)}, u32[]{:S(2)}) copy-start(s32[2]{0:T(128)S(1)} %subtract_bitcast_fusion.live_ref) | copy-start | bytes 28

commit v3 on v2

v3 whole, which is shorter than its diff:
```python
import functools
import math

import jax
import jax.numpy as jnp
from jax import lax
from jax.experimental import pallas as pl
from jax.experimental.pallas import tpu as pltpu
from jax.sharding import PartitionSpec as P

HEADS = 4
TILE = 128
HEAD_ROWS = 48
PART_ROWS = 40
ROW_STEP = 2048
SUB = 256
GATHER_STEP = 256
TABLE_PIECES = 8
STRIDE = 27
VMEM_LIMIT = 60 << 20
NEG_FILL = -1e30

VMEM = pl.BlockSpec(memory_space=pltpu.VMEM)
SMEM = pl.BlockSpec(memory_space=pltpu.SMEM)
ANY = pl.BlockSpec(memory_space=pl.ANY)
MESH = pl.DeviceIdType.MESH


def kernel(
    devices,
    slices,
    lengths,
    hist_source,
    cand_source,
    ids,
    table,
    w_query,
    w_key,
    w_value,
    w_out,
    out,
    wide,
    found,
    landing,
    scores_b,
    ids_landing,
    asked,
    rows_wide,
    cands,
    values,
    qt,
    parts,
    arrived,
    table_sem,
    asked_sem,
    ids_send,
    ids_recv,
    row_send,
    row_recv,
    cand_send,
    cand_recv,
    part_send,
    part_recv,
):
    f32, bf16 = jnp.float32, jnp.bfloat16
    me, my_slice = lax.axis_index("tbl"), lax.axis_index("tm")
    capacity, width = found.shape[1:]
    cand_block = cands.shape[1]
    requests, slice_len = hist_source.shape
    blocks = slices // requests
    items = blocks * HEADS
    head_dim = width // HEADS
    scale = 1.0 / math.sqrt(head_dim)
    to_exp2 = scale * math.log2(math.e)

    def forward(k):
        return lax.rem(me + k * STRIDE, devices)

    def backward(k):
        return lax.rem(me + k * (devices - STRIDE), devices)

    def other_slice(off):
        return lax.rem(my_slice + off, slices)

    per_piece = devices // TABLE_PIECES

    def table_copy(p):
        part = pl.ds(p * per_piece, per_piece)
        return pltpu.make_async_copy(table.at[part], found.at[part], table_sem.at[p])

    for p in range(TABLE_PIECES):
        table_copy(p).start()

    barrier = pltpu.get_barrier_semaphore()

    def greet(k, carry):
        pl.semaphore_signal(barrier, 1, device_id={"tbl": forward(k)}, device_id_type=MESH)
        return carry

    lax.fori_loop(1, devices, greet, 0)
    for off in range(1, slices):
        pl.semaphore_signal(barrier, 1, device_id={"tm": other_slice(off)}, device_id_type=MESH)
    pl.semaphore_wait(barrier, devices - 1 + slices - 1)

    def ids_copy(k):
        peer = forward(k)
        return pltpu.make_async_remote_copy(
            src_ref=ids.at[peer],
            dst_ref=ids_landing.at[me],
            send_sem=ids_send.at[k],
            recv_sem=ids_recv.at[k],
            device_id={"tbl": peer},
            device_id_type=MESH,
        )

    def send_ids(k, carry):
        ids_copy(k).start()
        return carry

    lax.fori_loop(1, devices, send_ids, 0)
    ids_landing[me] = ids[me]

    def widen(buffer, d):
        rows = pl.ds(pl.multiple_of(d * capacity, capacity), capacity)
        wide[rows, :] = buffer[d].astype(f32)

    for p in range(TABLE_PIECES):
        table_copy(p).wait()

        def widen_table(i, carry, p=p):
            widen(found, p * per_piece + i)
            return carry

        lax.fori_loop(0, per_piece, widen_table, 0)

    def wait_ids(k, carry):
        ids_copy(k).wait()
        return carry

    lax.fori_loop(1, devices, wait_ids, 0)
    listed = pltpu.make_async_copy(ids_landing, asked, asked_sem)
    listed.start()
    listed.wait()

    def look_up(k):
        peer = forward(k)

        def group(i, carry):
            for j in range(GATHER_STEP):
                row = asked[peer, i * (GATHER_STEP // TILE) + j // TILE, j % TILE]
                rows_wide[j : j + 1, :] = wide[pl.ds(row, 1), :]
            rows = pl.ds(pl.multiple_of(i * GATHER_STEP, GATHER_STEP), GATHER_STEP)
            found[k, rows, :] = rows_wide[...].astype(bf16)
            return carry

        lax.fori_loop(0, capacity // GATHER_STEP, group, 0)

    def row_copy(k):
        return pltpu.make_async_remote_copy(
            src_ref=found.at[k],
            dst_ref=landing.at[me],
            send_sem=row_send.at[k],
            recv_sem=row_recv.at[k],
            device_id={"tbl": forward(k)},
            device_id_type=MESH,
        )

    def send_rows(k, carry):
        look_up(k)
        row_copy(k).start()
        return carry

    lax.fori_loop(1, devices, send_rows, 0)
    look_up(0)
    own_rows = pl.ds(pl.multiple_of(me * capacity, capacity), capacity)
    wide[own_rows, :] = found[0].astype(f32)

    def take_rows(k, carry):
        row_copy(k).wait()
        widen(landing, backward(k))
        return carry

    lax.fori_loop(1, devices, take_rows, 0)

    def gather(pick):
        for j in range(GATHER_STEP):
            rows_wide[j : j + 1, :] = wide[pl.ds(pick(j), 1), :]
        return rows_wide[...].astype(bf16)

    def cand_group(i, carry):
        base = pl.multiple_of(i * GATHER_STEP, GATHER_STEP)
        cands[my_slice, pl.ds(base, GATHER_STEP), :] = gather(lambda j: cand_source[base + j])
        return carry

    lax.fori_loop(0, cand_block // GATHER_STEP, cand_group, 0)

    def cand_copy(off):
        return pltpu.make_async_remote_copy(
            src_ref=cands.at[my_slice],
            dst_ref=cands.at[my_slice],
            send_sem=cand_send.at[off],
            recv_sem=cand_recv.at[off],
            device_id={"tm": other_slice(off)},
            device_id_type=MESH,
        )

    for off in range(1, slices):
        cand_copy(off).start()

    pieces = slice_len // capacity
    halves = capacity // GATHER_STEP

    def hist_group(n, carry):
        r = n // (pieces * halves)
        base = pl.multiple_of(n % (pieces * halves) * GATHER_STEP, GATHER_STEP)
        rows = pl.ds(pl.multiple_of(n % halves * GATHER_STEP, GATHER_STEP), GATHER_STEP)
        found[n // halves, rows, :] = gather(lambda j: hist_source[r, base + j])
        return carry

    lax.fori_loop(0, requests * pieces * halves, hist_group, 0)
    for off in range(1, slices):
        cand_copy(off).wait()

    def part_copy(off, h):
        there = other_slice(off)
        return pltpu.make_async_remote_copy(
            src_ref=parts.at[there, h],
            dst_ref=arrived.at[my_slice, h],
            send_sem=part_send.at[off, h],
            recv_sem=part_recv.at[off, h],
            device_id={"tm": there},
            device_id_type=MESH,
        )

    head_of = lax.broadcasted_iota(jnp.int32, (width, cand_block), 0) // head_dim
    lowest = jnp.full((8, cand_block), -jnp.inf, f32)
    steps = slice_len // ROW_STEP
    lanes = cand_block // TILE
    subs = capacity // SUB

    def put_a(base, s):
        for c in range(lanes):
            wide[pl.ds(c * slice_len + base, SUB), :] = s[:, c * TILE : (c + 1) * TILE]

    def get_a(base):
        return jnp.concatenate(
            [wide[pl.ds(c * slice_len + base, SUB), :] for c in range(lanes)], axis=1
        )

    def put_b(base, s):
        scores_b[pl.ds(base, SUB), :] = s

    def get_b(base):
        return scores_b[pl.ds(base, SUB), :]

    def one_request(turn, carry):
        r = lax.rem(my_slice // blocks + 1 + turn, requests)
        live = lengths[r] - my_slice * slice_len

        def block_of(j):
            return r * blocks + lax.rem(my_slice + 1 + j, blocks)

        for b in range(blocks):
            query = jnp.dot(cands[block_of(b)], w_query[...], preferred_element_type=f32)
            turned = query.astype(bf16).astype(f32).T
            for h in range(HEADS):
                qt[b * HEADS + h] = jnp.where(head_of == h, turned, 0.0).astype(bf16)

        first_key = jnp.dot(found[r * pieces, 0:16, :], w_key[...], preferred_element_type=f32)[0:1]

        def project(i, c):
            rows = pl.ds(pl.multiple_of(i * capacity, capacity), capacity)
            x = found[r * pieces + i]
            key = jnp.dot(x, w_key[...], preferred_element_type=f32)
            down = lax.broadcasted_iota(jnp.int32, (capacity, width), 0) + i * capacity < live
            landing[i] = jnp.where(down, key, first_key).astype(bf16)
            turned = lax.dot_general(
                w_value[...], x, (((0,), (1,)), ((), ())), preferred_element_type=f32
            )
            visible = lax.broadcasted_iota(jnp.int32, (1, capacity), 1) + i * capacity < live
            turned = jnp.where(visible, turned, 0.0).astype(bf16)
            first = lax.broadcasted_iota(jnp.int32, (16, capacity), 0) == 0
            ones = jnp.where(first, jnp.where(visible, 1.0, 0.0), 0.0).astype(bf16)
            for h in range(HEADS):
                values[h, 0:head_dim, rows] = turned[h * head_dim : (h + 1) * head_dim]
                values[h, head_dim:HEAD_ROWS, rows] = ones
            return c

        lax.fori_loop(0, pieces, project, 0)

        def score(item, i, j, peak, put):
            keys = landing[i * (ROW_STEP // capacity) + j // subs, pl.ds(j % subs * SUB, SUB), :]
            s = jnp.dot(keys, qt[item], preferred_element_type=f32)
            put(pl.multiple_of(i * ROW_STEP + j * SUB, SUB), s)
            return jnp.maximum(peak, jnp.max(s.reshape(SUB // 8, 8, cand_block), axis=0))

        def first_scores(i, peak):
            for j in range(ROW_STEP // SUB):
                peak = score(0, i, j, peak, put_a)
            return peak

        def one_item(item, peak, get, put_next):
            top = jnp.max(peak, axis=0, keepdims=True)
            h = lax.rem(item, HEADS)
            following = jnp.minimum(item + 1, items - 1)

            def attend_step(i, c):
                next_peak, total = c
                for j in range(ROW_STEP // SUB):
                    base = pl.multiple_of(i * ROW_STEP + j * SUB, SUB)
                    next_peak = score(following, i, j, next_peak, put_next)
                    weights = jnp.exp2((get(base) - top) * to_exp2).astype(bf16)
                    total = total + jnp.dot(
                        values[h, :, pl.ds(base, SUB)], weights, preferred_element_type=f32
                    )
                return next_peak, total

            next_peak, total = lax.fori_loop(
                0, steps, attend_step, (lowest, jnp.zeros((HEAD_ROWS, cand_block), f32))
            )
            shown = jnp.where(live > 0, top * scale, NEG_FILL)
            row = lax.broadcasted_iota(jnp.int32, (8, cand_block), 0)
            tail = jnp.where(row == 1, shown, total[head_dim:PART_ROWS])
            there = block_of(item // HEADS)

            @pl.when(there != my_slice)
            def _():
                parts[there, h, 0:head_dim, :] = total[0:head_dim]
                parts[there, h, head_dim:PART_ROWS, :] = tail
                part_copy(lax.rem(there - my_slice + slices, slices), h).start()

            @pl.when(there == my_slice)
            def _():
                arrived[my_slice, h, 0:head_dim, :] = total[0:head_dim]
                arrived[my_slice, h, head_dim:PART_ROWS, :] = tail

            return next_peak

        def two_items(k, peak):
            peak = one_item(2 * k, peak, get_a, put_b)
            return one_item(2 * k + 1, peak, get_b, put_a)

        lax.fori_loop(0, items // 2, two_items, lax.fori_loop(0, steps, first_scores, lowest))
        return carry

    lax.fori_loop(0, requests, one_request, 0)
    for off in range(1, slices):
        for h in range(HEADS):
            part_copy(off, h).wait()

    heads = []
    for h in range(HEADS):
        peaks = [arrived[s, h, head_dim + 1 : head_dim + 2, :] for s in range(slices)]
        best = functools.reduce(jnp.maximum, peaks)
        denom = numer = 0.0
        for s in range(slices):
            rescale = jnp.exp(peaks[s] - best)
            denom = denom + rescale * arrived[s, h, head_dim : head_dim + 1, :]
            numer = numer + rescale * arrived[s, h, 0:head_dim, :]
        heads.append(numer / denom)
    attended = jnp.concatenate(heads, axis=0).T.astype(bf16)
    out[...] = jnp.dot(attended, w_out[...], preferred_element_type=f32).astype(out.dtype)


def shards(
    table,
    fetch_rows,
    tile_counts,
    hist_source,
    cand_source,
    lengths,
    w_query,
    w_key,
    w_value,
    w_out,
):
    del tile_counts
    devices, capacity = fetch_rows.shape[2:]
    slice_len = hist_source.shape[3]
    cand_block = cand_source.shape[2]
    width = table.shape[1]
    slices, tiles = lax.axis_size("tm"), capacity // TILE
    blocks = slices // hist_source.shape[2]
    f32, bf16 = jnp.float32, jnp.bfloat16
    rows = (devices, capacity, width)
    part = (slices, HEADS, PART_ROWS, cand_block)
    dma = pltpu.SemaphoreType.DMA
    return pl.pallas_call(
        functools.partial(kernel, devices, slices),
        out_shape=jax.ShapeDtypeStruct((cand_block, w_out.shape[1]), bf16),
        in_specs=[SMEM] * 3 + [VMEM, ANY] + [VMEM] * 4,
        out_specs=VMEM,
        scratch_shapes=[
            pltpu.VMEM(table.shape, f32),
            pltpu.VMEM(rows, bf16),
            pltpu.VMEM(rows, bf16),
            pltpu.VMEM((slice_len, cand_block), f32),
            pltpu.VMEM((devices, tiles, TILE), jnp.int32),
            pltpu.SMEM((devices, tiles, TILE), jnp.int32),
            pltpu.VMEM((GATHER_STEP, width), f32),
            pltpu.VMEM((slices, cand_block, width), bf16),
            pltpu.VMEM((HEADS, HEAD_ROWS, slice_len), bf16),
            pltpu.VMEM((blocks * HEADS, width, cand_block), bf16),
            pltpu.VMEM(part, f32),
            pltpu.VMEM(part, f32),
            dma((TABLE_PIECES,)),
            dma,
            dma((devices,)),
            dma((devices,)),
            dma((devices,)),
            dma((devices,)),
            dma((slices,)),
            dma((slices,)),
            dma((slices, HEADS)),
            dma((slices, HEADS)),
        ],
        compiler_params=pltpu.CompilerParams(
            collective_id=1, has_side_effects=True, vmem_limit_bytes=VMEM_LIMIT
        ),
        name="attend",
    )(
        lengths[0],
        hist_source[0, 0],
        cand_source[0, 0],
        fetch_rows.reshape(devices, tiles, TILE),
        table.reshape(rows),
        w_query,
        w_key,
        w_value,
        w_out,
    )


def solution(mesh):
    return jax.shard_map(
        shards,
        mesh=mesh,
        in_specs=(
            P("tbl", None),
            P("tbl", "tm", None, None),
            P("tbl", "tm", None),
            P("tbl", "tm", None, None),
            P("tbl", "tm", None),
            P("tbl", None),
            P(),
            P(),
            P(),
            P(),
        ),
        out_specs=P(("tbl", "tm"), None),
        check_vma=False,
    )
```

time: 309 us -> 325 us (1.052)
  Pallas kernels: 302 us -> 322 us
    pallas_call x2 -> x1, Pallas kernels: 302 us -> 322 us  [shards(): pl.pallas_call(functools.partial(kernel, devices, slices), out_shape=jax....]
where the time goes in v3:
time: 325 us
  Pallas kernels  322 us (99%)
    pallas_call x1, Pallas kernels, shards(): pl.pallas_call(functools.partial(kernel, devices, slices), out_shape=jax....  322 us

profile of v3, /device:TPU:32, one launch (start us, length us, event | category | flops | bytes accessed | tf_op | source)
XLA Modules:
  0.0 325.1 jit_solution(465977047516887914)
XLA Ops:
  0.0 1.6 reshape.6.ids
  1.6 321.9 %attend.1 = bf16[512,128]{1,0:T(8,128)(2,1)} custom-call(s32[2]{0:T(128)} %bitcast.9, s32[2,8192]{1,0:T(2,128)} %bitcast.7, s32[512]{0:T(512)} %bitcast.8, s32[64,4,128]{2,1,0:T(4,128)} %reshape.6.ids, bf16[64,512,128]{2,1,0:T(8,128)(2,1)} %bitcast.6, bf16[128,128]{1,0:T(8,128)(2,1)} %w_query.1, bf16[128,128]{1,0:T(8,128)(2,1)} %w_key.1, ...), custom_call_target="tpu_custom_call" | custom-call | tf_op jit(solution)/shard_map/attend/pallas_call | solution.py:388
  323.5 1.6 copy.11

commit v4 on v3

--- a/solution.py
+++ b/solution.py
@@ -17,7 +17,7 @@
 GATHER_STEP = 256
 TABLE_PIECES = 8
 STRIDE = 27
-VMEM_LIMIT = 60 << 20
+VMEM_LIMIT = 62 << 20
 NEG_FILL = -1e30
 
 VMEM = pl.BlockSpec(memory_space=pltpu.VMEM)
@@ -42,7 +42,7 @@
     wide,
     found,
     landing,
-    scores_b,
+    scores,
     ids_landing,
     asked,
     rows_wide,
@@ -66,7 +66,7 @@
     me, my_slice = lax.axis_index("tbl"), lax.axis_index("tm")
     capacity, width = found.shape[1:]
     cand_block = cands.shape[1]
-    requests, slice_len = hist_source.shape
+    requests, slice_len = lengths.shape[0], hist_source.size // lengths.shape[0]
     blocks = slices // requests
     items = blocks * HEADS
     head_dim = width // HEADS
@@ -209,15 +209,21 @@
 
     pieces = slice_len // capacity
     halves = capacity // GATHER_STEP
-
-    def hist_group(n, carry):
-        r = n // (pieces * halves)
-        base = pl.multiple_of(n % (pieces * halves) * GATHER_STEP, GATHER_STEP)
-        rows = pl.ds(pl.multiple_of(n % halves * GATHER_STEP, GATHER_STEP), GATHER_STEP)
-        found[n // halves, rows, :] = gather(lambda j: hist_source[r, base + j])
-        return carry
-
-    lax.fori_loop(0, requests * pieces * halves, hist_group, 0)
+    order = [lax.rem(my_slice // blocks + 1 + turn, requests) for turn in range(requests)]
+
+    def hist_piece(r, i):
+        piece = r * pieces + i
+        for half in range(halves):
+            first = (piece * halves + half) * (GATHER_STEP // TILE)
+            found[piece, half * GATHER_STEP : (half + 1) * GATHER_STEP, :] = gather(
+                lambda j: hist_source[first + j // TILE, j % TILE]
+            )
+
+    def first_history(i, carry):
+        hist_piece(order[0], i)
+        return carry
+
+    lax.fori_loop(0, pieces, first_history, 0)
     for off in range(1, slices):
         cand_copy(off).wait()
 
@@ -235,37 +241,27 @@
     head_of = lax.broadcasted_iota(jnp.int32, (width, cand_block), 0) // head_dim
     lowest = jnp.full((8, cand_block), -jnp.inf, f32)
     steps = slice_len // ROW_STEP
-    lanes = cand_block // TILE
     subs = capacity // SUB
-
-    def put_a(base, s):
-        for c in range(lanes):
-            wide[pl.ds(c * slice_len + base, SUB), :] = s[:, c * TILE : (c + 1) * TILE]
-
-    def get_a(base):
-        return jnp.concatenate(
-            [wide[pl.ds(c * slice_len + base, SUB), :] for c in range(lanes)], axis=1
-        )
-
-    def put_b(base, s):
-        scores_b[pl.ds(base, SUB), :] = s
-
-    def get_b(base):
-        return scores_b[pl.ds(base, SUB), :]
-
-    def one_request(turn, carry):
+    last = requests * items - 1
+
+    def block_of(item):
+        turn, j = item // items, item % items // HEADS
         r = lax.rem(my_slice // blocks + 1 + turn, requests)
+        return r, r * blocks + lax.rem(my_slice + 1 + j, blocks)
+
+    def one_block(n, carry):
+        _, block = block_of(n * HEADS)
+        query = jnp.dot(cands[block], w_query[...], preferred_element_type=f32)
+        turned = query.astype(bf16).astype(f32).T
+        for h in range(HEADS):
+            qt[n * HEADS + h] = jnp.where(head_of == h, turned, 0.0).astype(bf16)
+        return carry
+
+    lax.fori_loop(0, slices, one_block, 0)
+
+    def project_request(turn):
+        r = order[turn]
         live = lengths[r] - my_slice * slice_len
-
-        def block_of(j):
-            return r * blocks + lax.rem(my_slice + 1 + j, blocks)
-
-        for b in range(blocks):
-            query = jnp.dot(cands[block_of(b)], w_query[...], preferred_element_type=f32)
-            turned = query.astype(bf16).astype(f32).T
-            for h in range(HEADS):
-                qt[b * HEADS + h] = jnp.where(head_of == h, turned, 0.0).astype(bf16)
-
         first_key = jnp.dot(found[r * pieces, 0:16, :], w_key[...], preferred_element_type=f32)[0:1]
 
         def project(i, c):
@@ -273,7 +269,7 @@
             x = found[r * pieces + i]
             key = jnp.dot(x, w_key[...], preferred_element_type=f32)
             down = lax.broadcasted_iota(jnp.int32, (capacity, width), 0) + i * capacity < live
-            landing[i] = jnp.where(down, key, first_key).astype(bf16)
+            landing[turn * pieces + i] = jnp.where(down, key, first_key).astype(bf16)
             turned = lax.dot_general(
                 w_value[...], x, (((0,), (1,)), ((), ())), preferred_element_type=f32
             )
@@ -282,68 +278,84 @@
             first = lax.broadcasted_iota(jnp.int32, (16, capacity), 0) == 0
             ones = jnp.where(first, jnp.where(visible, 1.0, 0.0), 0.0).astype(bf16)
             for h in range(HEADS):
-                values[h, 0:head_dim, rows] = turned[h * head_dim : (h + 1) * head_dim]
-                values[h, head_dim:HEAD_ROWS, rows] = ones
+                at = turn * HEADS + h
+                values[at, 0:head_dim, rows] = turned[h * head_dim : (h + 1) * head_dim]
+                values[at, head_dim:HEAD_ROWS, rows] = ones
             return c
 
         lax.fori_loop(0, pieces, project, 0)
 
-        def score(item, i, j, peak, put):
-            keys = landing[i * (ROW_STEP // capacity) + j // subs, pl.ds(j % subs * SUB, SUB), :]
-            s = jnp.dot(keys, qt[item], preferred_element_type=f32)
-            put(pl.multiple_of(i * ROW_STEP + j * SUB, SUB), s)
-            return jnp.maximum(peak, jnp.max(s.reshape(SUB // 8, 8, cand_block), axis=0))
-
-        def first_scores(i, peak):
+    def score(item, i, j):
+        piece = item // items * pieces + i * (ROW_STEP // capacity) + j // subs
+        keys = landing[piece, pl.ds(j % subs * SUB, SUB), :]
+        return jnp.dot(keys, qt[item], preferred_element_type=f32)
+
+    def raised(peak, s):
+        return jnp.maximum(peak, jnp.max(s.reshape(SUB // 8, 8, cand_block), axis=0))
+
+    def step_scores(i):
+        return scores.at[pl.ds(pl.multiple_of(i * ROW_STEP, ROW_STEP), ROW_STEP)]
+
+    def first_scores(i, peak):
+        held = step_scores(i)
+        for j in range(ROW_STEP // SUB):
+            s = score(0, i, j)
+            held[j * SUB : (j + 1) * SUB, :] = s
+            peak = raised(peak, s)
+        return peak
+
+    def one_item(item, peak, beside=None, follow=True):
+        top = jnp.max(peak, axis=0, keepdims=True)
+        at = item // items * HEADS + item % HEADS
+
+        def attend_step(i, c):
+            next_peak, total = c
+            held = step_scores(i)
+            if beside is not None:
+                beside(item * steps + i)
             for j in range(ROW_STEP // SUB):
-                peak = score(0, i, j, peak, put_a)
-            return peak
-
-        def one_item(item, peak, get, put_next):
-            top = jnp.max(peak, axis=0, keepdims=True)
-            h = lax.rem(item, HEADS)
-            following = jnp.minimum(item + 1, items - 1)
-
-            def attend_step(i, c):
-                next_peak, total = c
-                for j in range(ROW_STEP // SUB):
-                    base = pl.multiple_of(i * ROW_STEP + j * SUB, SUB)
-                    next_peak = score(following, i, j, next_peak, put_next)
-                    weights = jnp.exp2((get(base) - top) * to_exp2).astype(bf16)
-                    total = total + jnp.dot(
-                        values[h, :, pl.ds(base, SUB)], weights, preferred_element_type=f32
-                    )
-                return next_peak, total
-
-            next_peak, total = lax.fori_loop(
-                0, steps, attend_step, (lowest, jnp.zeros((HEAD_ROWS, cand_block), f32))
-            )
-            shown = jnp.where(live > 0, top * scale, NEG_FILL)
-            row = lax.broadcasted_iota(jnp.int32, (8, cand_block), 0)
-            tail = jnp.where(row == 1, shown, total[head_dim:PART_ROWS])
-            there = block_of(item // HEADS)
-
-            @pl.when(there != my_slice)
-            def _():
-                parts[there, h, 0:head_dim, :] = total[0:head_dim]
-                parts[there, h, head_dim:PART_ROWS, :] = tail
-                part_copy(lax.rem(there - my_slice + slices, slices), h).start()
-
-            @pl.when(there == my_slice)
-            def _():
-                arrived[my_slice, h, 0:head_dim, :] = total[0:head_dim]
-                arrived[my_slice, h, head_dim:PART_ROWS, :] = tail
-
-            return next_peak
-
-        def two_items(k, peak):
-            peak = one_item(2 * k, peak, get_a, put_b)
-            return one_item(2 * k + 1, peak, get_b, put_a)
-
-        lax.fori_loop(0, items // 2, two_items, lax.fori_loop(0, steps, first_scores, lowest))
-        return carry
-
-    lax.fori_loop(0, requests, one_request, 0)
+                part = slice(j * SUB, (j + 1) * SUB)
+                rows = pl.ds(pl.multiple_of(i * ROW_STEP + j * SUB, SUB), SUB)
+                weights = jnp.exp2((held[part, :] - top) * to_exp2).astype(bf16)
+                if follow:
+                    s = score(item + 1, i, j)
+                    held[part, :] = s
+                    next_peak = raised(next_peak, s)
+                total = total + jnp.dot(values[at, :, rows], weights, preferred_element_type=f32)
+            return next_peak, total
+
+        next_peak, total = lax.fori_loop(
+            0, steps, attend_step, (lowest, jnp.zeros((HEAD_ROWS, cand_block), f32))
+        )
+        r, there = block_of(item)
+        h = item % HEADS
+        live = lengths[r] - my_slice * slice_len
+        shown = jnp.where(live > 0, top * scale, NEG_FILL)
+        row = lax.broadcasted_iota(jnp.int32, (8, cand_block), 0)
+        tail = jnp.where(row == 1, shown, total[head_dim:PART_ROWS])
+
+        @pl.when(there != my_slice)
+        def _():
+            parts[there, h, 0:head_dim, :] = total[0:head_dim]
+            parts[there, h, head_dim:PART_ROWS, :] = tail
+            part_copy(lax.rem(there - my_slice + slices, slices), h).start()
+
+        @pl.when(there == my_slice)
+        def _():
+            arrived[my_slice, h, 0:head_dim, :] = total[0:head_dim]
+            arrived[my_slice, h, head_dim:PART_ROWS, :] = tail
+
+        return next_peak
+
+    project_request(0)
+    peak = lax.fori_loop(0, steps, first_scores, lowest)
+    early = pieces // steps
+    peak = lax.fori_loop(
+        0, early, lambda n, p: one_item(n, p, beside=lambda i: hist_piece(order[1], i)), peak
+    )
+    project_request(1)
+    peak = lax.fori_loop(early, last, one_item, peak)
+    one_item(last, peak, follow=False)
     for off in range(1, slices):
         for h in range(HEADS):
             part_copy(off, h).wait()
@@ -380,7 +392,7 @@
     cand_block = cand_source.shape[2]
     width = table.shape[1]
     slices, tiles = lax.axis_size("tm"), capacity // TILE
-    blocks = slices // hist_source.shape[2]
+    requests = hist_source.shape[2]
     f32, bf16 = jnp.float32, jnp.bfloat16
     rows = (devices, capacity, width)
     part = (slices, HEADS, PART_ROWS, cand_block)
@@ -399,8 +411,8 @@
             pltpu.SMEM((devices, tiles, TILE), jnp.int32),
             pltpu.VMEM((GATHER_STEP, width), f32),
             pltpu.VMEM((slices, cand_block, width), bf16),
-            pltpu.VMEM((HEADS, HEAD_ROWS, slice_len), bf16),
-            pltpu.VMEM((blocks * HEADS, width, cand_block), bf16),
+            pltpu.VMEM((requests * HEADS, HEAD_ROWS, slice_len), bf16),
+            pltpu.VMEM((slices * HEADS, width, cand_block), bf16),
             pltpu.VMEM(part, f32),
             pltpu.VMEM(part, f32),
             dma((TABLE_PIECES,)),
@@ -420,7 +432,7 @@
         name="attend",
     )(
         lengths[0],
-        hist_source[0, 0],
+        hist_source.reshape(-1, TILE),
         cand_source[0, 0],
         fetch_rows.reshape(devices, tiles, TILE),
         table.reshape(rows),

time: 325 us -> 301 us (0.926)
  Pallas kernels: 322 us -> 296 us
    pallas_call x1, Pallas kernels: 322 us -> 296 us  [shards(): pl.pallas_call(functools.partial(kernel, devices, slices), out_shape=jax....]
where the time goes in v4:
time: 301 us
  Pallas kernels  296 us (98%)
  local copies, waits for them, and re-layouts  4.68 us (2%)
    pallas_call x1, Pallas kernels, shards(): pl.pallas_call(functools.partial(kernel, devices, slices), out_shape=jax....  296 us

profile of v4, /device:TPU:32, one launch (start us, length us, event | category | flops | bytes accessed | tf_op | source)
XLA Modules:
  0.0 301.0 jit_solution(5236279647605945915)
XLA Ops:
  0.0 1.5 reshape.9.hist_source
  1.5 1.6 reshape.10.ids
  3.1 296.3 %attend.1 = bf16[512,128]{1,0:T(8,128)(2,1)} custom-call(s32[2]{0:T(128)} %bitcast.7, s32[128,128]{1,0:T(8,128)} %reshape.9.hist_source, s32[512]{0:T(512)} %bitcast.6, s32[64,4,128]{2,1,0:T(4,128)} %reshape.10.ids, bf16[64,512,128]{2,1,0:T(8,128)(2,1)} %bitcast.5, bf16[128,128]{1,0:T(8,128)(2,1)} %w_query.1, bf16[128,128]{1,0:T(8,128)(2,1)} %w_key.1, ...), custom_call_target="tpu_custom_call" | custom-call | tf_op jit(solution)/shard_map/attend/pallas_call | solution.py:400
  299.4 1.6 copy.11

commit v5 on v4

--- a/solution.py
+++ b/solution.py
@@ -16,6 +16,7 @@
 SUB = 256
 GATHER_STEP = 256
 TABLE_PIECES = 8
+ID_BATCHES = 4
 STRIDE = 27
 VMEM_LIMIT = 62 << 20
 NEG_FILL = -1e30
@@ -103,10 +104,10 @@
     pl.semaphore_wait(barrier, devices - 1 + slices - 1)
 
     def ids_copy(k):
-        peer = forward(k)
+        peer = backward(k)
         return pltpu.make_async_remote_copy(
             src_ref=ids.at[peer],
-            dst_ref=ids_landing.at[me],
+            dst_ref=ids_landing.at[k],
             send_sem=ids_send.at[k],
             recv_sem=ids_recv.at[k],
             device_id={"tbl": peer},
@@ -118,7 +119,7 @@
         return carry
 
     lax.fori_loop(1, devices, send_ids, 0)
-    ids_landing[me] = ids[me]
+    ids_landing[0] = ids[me]
 
     def widen(buffer, d):
         rows = pl.ds(pl.multiple_of(d * capacity, capacity), capacity)
@@ -137,20 +138,23 @@
         ids_copy(k).wait()
         return carry
 
-    lax.fori_loop(1, devices, wait_ids, 0)
-    listed = pltpu.make_async_copy(ids_landing, asked, asked_sem)
-    listed.start()
-    listed.wait()
+    per_batch = devices // ID_BATCHES
+
+    def list_copy(n):
+        part = pl.ds(n * per_batch, per_batch)
+        return pltpu.make_async_copy(ids_landing.at[part], asked.at[part], asked_sem.at[n])
+
+    for n in range(ID_BATCHES):
+        lax.fori_loop(max(1, n * per_batch), (n + 1) * per_batch, wait_ids, 0)
+        list_copy(n).start()
 
     def look_up(k):
-        peer = forward(k)
-
         def group(i, carry):
             for j in range(GATHER_STEP):
-                row = asked[peer, i * (GATHER_STEP // TILE) + j // TILE, j % TILE]
+                row = asked[k, i * (GATHER_STEP // TILE) + j // TILE, j % TILE]
                 rows_wide[j : j + 1, :] = wide[pl.ds(row, 1), :]
             rows = pl.ds(pl.multiple_of(i * GATHER_STEP, GATHER_STEP), GATHER_STEP)
-            found[k, rows, :] = rows_wide[...].astype(bf16)
+            found[k, rows, :] = rows_wide[0:GATHER_STEP, :].astype(bf16)
             return carry
 
         lax.fori_loop(0, capacity // GATHER_STEP, group, 0)
@@ -170,7 +174,9 @@
         row_copy(k).start()
         return carry
 
-    lax.fori_loop(1, devices, send_rows, 0)
+    for n in range(ID_BATCHES):
+        list_copy(n).wait()
+        lax.fori_loop(max(1, n * per_batch), (n + 1) * per_batch, send_rows, 0)
     look_up(0)
     own_rows = pl.ds(pl.multiple_of(me * capacity, capacity), capacity)
     wide[own_rows, :] = found[0].astype(f32)
@@ -185,7 +191,7 @@
     def gather(pick):
         for j in range(GATHER_STEP):
             rows_wide[j : j + 1, :] = wide[pl.ds(pick(j), 1), :]
-        return rows_wide[...].astype(bf16)
+        return rows_wide[0:GATHER_STEP, :].astype(bf16)
 
     def cand_group(i, carry):
         base = pl.multiple_of(i * GATHER_STEP, GATHER_STEP)
@@ -311,9 +317,9 @@
         def attend_step(i, c):
             next_peak, total = c
             held = step_scores(i)
-            if beside is not None:
-                beside(item * steps + i)
             for j in range(ROW_STEP // SUB):
+                if beside is not None:
+                    beside(item * steps + i, j)
                 part = slice(j * SUB, (j + 1) * SUB)
                 rows = pl.ds(pl.multiple_of(i * ROW_STEP + j * SUB, SUB), SUB)
                 weights = jnp.exp2((held[part, :] - top) * to_exp2).astype(bf16)
@@ -350,9 +356,17 @@
     project_request(0)
     peak = lax.fori_loop(0, steps, first_scores, lowest)
     early = pieces // steps
-    peak = lax.fori_loop(
-        0, early, lambda n, p: one_item(n, p, beside=lambda i: hist_piece(order[1], i)), peak
-    )
+    few = capacity // (ROW_STEP // SUB)
+
+    def gather_few(i, j):
+        piece = order[1] * pieces + i
+        part = slice(j * few, (j + 1) * few)
+        for n in range(j * few, (j + 1) * few):
+            row = hist_source[piece * (capacity // TILE) + n // TILE, n % TILE]
+            rows_wide[n : n + 1, :] = wide[pl.ds(row, 1), :]
+        found[piece, part, :] = rows_wide[part, :].astype(bf16)
+
+    peak = lax.fori_loop(0, early, lambda n, p: one_item(n, p, beside=gather_few), peak)
     project_request(1)
     peak = lax.fori_loop(early, last, one_item, peak)
     one_item(last, peak, follow=False)
@@ -409,14 +423,14 @@
             pltpu.VMEM((slice_len, cand_block), f32),
             pltpu.VMEM((devices, tiles, TILE), jnp.int32),
             pltpu.SMEM((devices, tiles, TILE), jnp.int32),
-            pltpu.VMEM((GATHER_STEP, width), f32),
+            pltpu.VMEM((capacity, width), f32),
             pltpu.VMEM((slices, cand_block, width), bf16),
             pltpu.VMEM((requests * HEADS, HEAD_ROWS, slice_len), bf16),
             pltpu.VMEM((slices * HEADS, width, cand_block), bf16),
             pltpu.VMEM(part, f32),
             pltpu.VMEM(part, f32),
             dma((TABLE_PIECES,)),
-            dma,
+            dma((ID_BATCHES,)),
             dma((devices,)),
             dma((devices,)),
             dma((devices,)),

time: 301 us -> 298 us (0.990)
    pallas_call x1, Pallas kernels: 296 us -> 293 us  [shards(): pl.pallas_call(functools.partial(kernel, devices, slices), out_shape=jax....]
where the time goes in v5:
time: 298 us
  Pallas kernels  293 us (98%)
  local copies, waits for them, and re-layouts  4.68 us (2%)
    pallas_call x1, Pallas kernels, shards(): pl.pallas_call(functools.partial(kernel, devices, slices), out_shape=jax....  293 us

profile of v5, /device:TPU:32, one launch (start us, length us, event | category | flops | bytes accessed | tf_op | source)
XLA Modules:
  0.0 297.9 jit_solution(9669025087839306067)
XLA Ops:
  0.0 1.5 reshape.9.hist_source
  1.5 1.6 reshape.10.ids
  3.1 293.2 %attend.1 = bf16[512,128]{1,0:T(8,128)(2,1)} custom-call(s32[2]{0:T(128)} %bitcast.7, s32[128,128]{1,0:T(8,128)} %reshape.9.hist_source, s32[512]{0:T(512)} %bitcast.6, s32[64,4,128]{2,1,0:T(4,128)} %reshape.10.ids, bf16[64,512,128]{2,1,0:T(8,128)(2,1)} %bitcast.5, bf16[128,128]{1,0:T(8,128)(2,1)} %w_query.1, bf16[128,128]{1,0:T(8,128)(2,1)} %w_key.1, ...), custom_call_target="tpu_custom_call" | custom-call | tf_op jit(solution)/shard_map/attend/pallas_call | solution.py:414
  296.3 1.6 copy.11

commit v6 on v5

--- a/solution.py
+++ b/solution.py
@@ -12,7 +12,8 @@
 TILE = 128
 HEAD_ROWS = 48
 PART_ROWS = 40
-ROW_STEP = 2048
+ROW_STEP = 4096
+BESIDE = 64
 SUB = 256
 GATHER_STEP = 256
 TABLE_PIECES = 8
@@ -355,15 +356,17 @@
 
     project_request(0)
     peak = lax.fori_loop(0, steps, first_scores, lowest)
-    early = pieces // steps
-    few = capacity // (ROW_STEP // SUB)
+    shares = capacity // BESIDE
+    per_step = ROW_STEP // SUB // shares
+    early = pieces // steps // per_step
 
     def gather_few(i, j):
-        piece = order[1] * pieces + i
-        part = slice(j * few, (j + 1) * few)
-        for n in range(j * few, (j + 1) * few):
+        piece = order[1] * pieces + i * per_step + j // shares
+        start = j % shares * BESIDE
+        for n in range(start, start + BESIDE):
             row = hist_source[piece * (capacity // TILE) + n // TILE, n % TILE]
             rows_wide[n : n + 1, :] = wide[pl.ds(row, 1), :]
+        part = slice(start, start + BESIDE)
         found[piece, part, :] = rows_wide[part, :].astype(bf16)
 
     peak = lax.fori_loop(0, early, lambda n, p: one_item(n, p, beside=gather_few), peak)

time: 298 us -> 293 us (0.983)
  Pallas kernels: 293 us -> 288 us
    pallas_call x1, Pallas kernels: 293 us -> 288 us  [shards(): pl.pallas_call(functools.partial(kernel, devices, slices), out_shape=jax....]
where the time goes in v6:
time: 293 us
  Pallas kernels  288 us (98%)
  local copies, waits for them, and re-layouts  4.68 us (2%)
    pallas_call x1, Pallas kernels, shards(): pl.pallas_call(functools.partial(kernel, devices, slices), out_shape=jax....  288 us

profile of v6, /device:TPU:32, one launch (start us, length us, event | category | flops | bytes accessed | tf_op | source)
XLA Modules:
  0.0 292.7 jit_solution(5214897668537940955)
XLA Ops:
  0.0 1.5 reshape.9.hist_source
  1.5 1.6 reshape.10.ids
  3.1 288.0 %attend.1 = bf16[512,128]{1,0:T(8,128)(2,1)} custom-call(s32[2]{0:T(128)} %bitcast.7, s32[128,128]{1,0:T(8,128)} %reshape.9.hist_source, s32[512]{0:T(512)} %bitcast.6, s32[64,4,128]{2,1,0:T(4,128)} %reshape.10.ids, bf16[64,512,128]{2,1,0:T(8,128)(2,1)} %bitcast.5, bf16[128,128]{1,0:T(8,128)(2,1)} %w_query.1, bf16[128,128]{1,0:T(8,128)(2,1)} %w_key.1, ...), custom_call_target="tpu_custom_call" | custom-call | tf_op jit(solution)/shard_map/attend/pallas_call | solution.py:417
  291.1 1.6 copy.11
